TPU v7x, 256 devices: a whole 4x4x8 slice. The times are simulated.
256 devices in a mesh: dp: 2 (over core), seq: 8 (over z), expert: 16 (over y, x).
Axes of the slice: x: 4, y: 4, z: 8, core: 2. Of those that a mesh axis runs over, the one named last changes fastest.
Arguments:
- tokens: bfloat16 [16, 2048, 2560], P(('dp', 'seq'), 'expert'), may hold values from -6 to 6
- text_states: bfloat16 [16, 128, 4096], P('dp', None, 'seq'), may hold values from -6 to 6
- text_lengths: int32 [16], P('dp'), may hold values from 64 to 128
- mod_weight: bfloat16 [4096, 5120], P('seq', 'expert'), may hold values from -1 to 1
- router_weight: bfloat16 [2560, 4], replicated, may hold values from -0.125 to 0.125
- gate_weight: bfloat16 [2560, 13824], P('dp', 'expert'), may hold values from -0.125 to 0.125
- up_weight: bfloat16 [2560, 13824], P('dp', 'expert'), may hold values from -0.125 to 0.125
- down_weight: bfloat16 [13824, 2560], P('expert', 'dp'), may hold values from -0.109375 to 0.109375
- expert_ids: int32 [16, 2048, 2], P(('dp', 'seq'), 'expert'), may hold values from 0 to 3, all different within a row; in each aligned block of 128 rows (0 to 127, 128 to 255, ..., all dimensions but the last counted through in order) at most 68 rows name the same one
- dropped: int32 [16, 2048, 2], P(('dp', 'seq'), 'expert'), may hold values 0 or 1
Outputs:
- mixed: bfloat16 [16, 2048, 2560], P(('dp', 'seq'), 'expert')
Inputs may be any that keep to these rules, and one draw needn't show every extreme that they name: `expert_ids`: each row names 2 different experts. In every aligned block of 128 patches (one image's patches on one device) no expert is named by more than 68 rows, and some block reaches 68.
All inputs are finite; a program needn't handle non-finite values. No bound on the sum of `dropped` on one device may be relied on, other than what follows from the above.
Results may differ from a plain program's by a relative error of at most 0.014.
Values may be sent and summed in bfloat16 or wider, within the bound.
No kernel may reach another device: no remote copies, remote signals or barrier semaphores. Data moves between devices by JAX's collectives and lax.ppermute only.
A program may use at most 128 MiB of HBM per device.

v0:
```python
import functools

import jax
import jax.numpy as jnp
from jax import lax
from jax.experimental import pallas as pl
from jax.experimental.pallas import tpu as pltpu
from jax.sharding import PartitionSpec as P

SIDE = 4
SLOTS = 72
MOST = 68
OFFSETS = (0, 1, -1, 2)
BAND = 256
VMEM_LIMIT = 20 * 1024 * 1024
TRANSPOSED = (((1,), (1,)), ((), ()))


def along_x(step):
    return [
        (y * SIDE + x, y * SIDE + (x + step) % SIDE) for y in range(SIDE) for x in range(SIDE)
    ]


def along_y(step):
    return [
        (y * SIDE + x, ((y + step) % SIDE) * SIDE + x) for y in range(SIDE) for x in range(SIDE)
    ]


def shift(value, perm):
    return lax.ppermute(value, "expert", perm)


def after(value, *others):
    return lax.optimization_barrier((value,) + others)[0]


def in_vmem():
    return pl.BlockSpec(memory_space=pltpu.VMEM)


def in_smem():
    return pl.BlockSpec(memory_space=pltpu.SMEM)


def ranks(y_ref, ids_ref):
    rows = ids_ref.shape[1]
    before = (
        lax.broadcasted_iota(jnp.int32, (rows, rows), 0)
        < lax.broadcasted_iota(jnp.int32, (rows, rows), 1)
    ).astype(jnp.bfloat16)
    place = lax.broadcasted_iota(jnp.int32, (8, rows), 0)
    expert = jnp.full((8, rows), -1, jnp.int32)
    for k, offset in enumerate(OFFSETS):
        expert = jnp.where(place == k, lax.rem(y_ref[0] + offset + SIDE, SIDE), expert)
    named = jnp.where((ids_ref[0:1, :] == expert) | (ids_ref[1:2, :] == expert), 1.0, 0.0)
    rank = jnp.dot(named.astype(jnp.bfloat16), before, preferred_element_type=jnp.float32)
    return jnp.where(named > 0.0, rank, -1.0)


def bin_kernel(y_ref, ids_ref, tokens_ref, normed_ref, *bin_refs):
    rows, width = tokens_ref.shape
    for start in range(0, rows, 16):
        block = tokens_ref[start : start + 16, :].astype(jnp.float32)
        centre = jnp.sum(block, axis=1, keepdims=True) * (1.0 / width)
        block = block - centre
        spread = jnp.sum(block * block, axis=1, keepdims=True) * (1.0 / width)
        normed_ref[start : start + 16, :] = (block * lax.rsqrt(spread + 1e-06)).astype(
            jnp.bfloat16
        )
    rank = ranks(y_ref, ids_ref)
    slot = lax.broadcasted_iota(jnp.int32, (SLOTS, rows), 0).astype(jnp.float32)
    normed = normed_ref[...]
    for k, bin_ref in enumerate(bin_refs):
        pick = jnp.where(slot == rank[k : k + 1, :], 1.0, 0.0).astype(jnp.bfloat16)
        for half in range(2):
            span = slice(half * (width // 2), (half + 1) * (width // 2))
            bin_ref[half] = jnp.dot(
                pick, normed[:, span], preferred_element_type=jnp.float32
            ).astype(jnp.bfloat16)


def make_bins(y_index, ids_rows, tokens):
    rows, width = tokens.shape
    return pl.pallas_call(
        bin_kernel,
        out_shape=[jax.ShapeDtypeStruct((rows, width), jnp.bfloat16)]
        + [jax.ShapeDtypeStruct((2, SLOTS, width // 2), jnp.bfloat16)] * len(OFFSETS),
        in_specs=[in_smem(), in_vmem(), in_vmem()],
        out_specs=[in_vmem()] * (1 + len(OFFSETS)),
        compiler_params=pltpu.CompilerParams(vmem_limit_bytes=VMEM_LIMIT),
        cost_estimate=pl.CostEstimate(
            flops=2 * 4 * SLOTS * rows * width, bytes_accessed=8 * rows * width, transcendentals=0
        ),
        name="normalise_and_bin",
    )(y_index, ids_rows, tokens)


def pack_kernel(first_ref, second_ref, out_ref):
    row = lax.broadcasted_iota(jnp.int32, (2 * MOST, SLOTS), 0)
    column = lax.broadcasted_iota(jnp.int32, (2 * MOST, SLOTS), 1)
    first = ((row == column) & (row < MOST)).astype(jnp.bfloat16)
    second = (row == column + MOST).astype(jnp.bfloat16)
    for side in range(2):
        out_ref[side] = (
            jnp.dot(first, first_ref[side], preferred_element_type=jnp.float32)
            + jnp.dot(second, second_ref[side], preferred_element_type=jnp.float32)
        ).astype(jnp.bfloat16)


def pack(first, second):
    _, slots, half = first.shape
    return pl.pallas_call(
        pack_kernel,
        out_shape=jax.ShapeDtypeStruct((2, 2 * MOST, half), jnp.bfloat16),
        in_specs=[in_vmem()] * 2,
        out_specs=in_vmem(),
        compiler_params=pltpu.CompilerParams(vmem_limit_bytes=VMEM_LIMIT),
        cost_estimate=pl.CostEstimate(
            flops=16 * MOST * slots * half, bytes_accessed=16 * MOST * half, transcendentals=0
        ),
        name="pack",
    )(first, second)


def expert_kernel(
    dp_ref,
    mod_ref,
    own_ref,
    left_ref,
    right_ref,
    *refs,
):
    *far_refs, gate_own, gate_far, up_own, up_far, down_own, down_far = refs[:-6]
    out_own, out_left, out_right, out_far, hidden_in, hidden = refs[-6:]
    _, size, half = own_ref.shape
    units = gate_own.shape[0]
    banks = (dp_ref[0], 1 - dp_ref[0])
    for side in range(2):
        far_ref = far_refs[side] if len(far_refs) == 2 else far_refs[0].at[side]

        def prepare(step, carry, side=side, far_ref=far_ref):
            start = pl.multiple_of(step * BAND, BAND)
            span = pl.ds(start, BAND)
            column = pl.ds(pl.multiple_of(side * half + start, BAND), BAND)
            blocks = [ref[side, :, span] for ref in (own_ref, left_ref, right_ref)]
            values = jnp.concatenate(
                [block.astype(jnp.float32) for block in blocks + [far_ref[:, span]]], axis=0
            )
            hidden_in[banks[side], :, span] = (
                values * (1.0 + mod_ref[0:1, column]) + mod_ref[1:2, column]
            ).astype(jnp.bfloat16)
            return carry

        lax.fori_loop(0, half // BAND, prepare, 0)

    def band(start, count):
        span = pl.ds(start, count)
        both = 0.0
        for bank, (gate, up) in enumerate(((gate_own, up_own), (gate_far, up_far))):
            both = both + lax.dot_general(
                hidden_in[bank],
                jnp.concatenate([gate[span, :], up[span, :]], axis=0),
                TRANSPOSED,
                preferred_element_type=jnp.float32,
            )
        hidden[:, span] = (jax.nn.silu(both[:, :count]) * both[:, count:]).astype(jnp.bfloat16)

    def full_band(step, carry):
        band(pl.multiple_of(step * BAND, BAND), BAND)
        return carry

    lax.fori_loop(0, units // BAND, full_band, 0)
    if units % BAND:
        band(units - units % BAND, units % BAND)
    tile = half // 2
    outs = (out_own, out_left, out_right, out_far)
    for bank, down in enumerate((down_own, down_far)):

        def project(step, carry, bank=bank, down=down):
            span = pl.ds(pl.multiple_of(step * tile, tile), tile)
            out = jnp.dot(hidden[...], down[:, span], preferred_element_type=jnp.float32)
            for k, out_ref in enumerate(outs):
                out_ref[banks[bank], :, span] = out[k * size : (k + 1) * size].astype(
                    jnp.bfloat16
                )
            return carry

        lax.fori_loop(0, half // tile, project, 0)


def run_expert(dp_index, modulation, own, left, right, fars, weights):
    _, size, half = own.shape
    units = weights[0].shape[0]
    rows = SIDE * size
    return pl.pallas_call(
        expert_kernel,
        out_shape=[jax.ShapeDtypeStruct(own.shape, jnp.bfloat16)] * 4,
        in_specs=[in_smem()] + [in_vmem()] * (4 + len(fars) + len(weights)),
        out_specs=[in_vmem()] * 4,
        scratch_shapes=[
            pltpu.VMEM((2, rows, half), jnp.bfloat16),
            pltpu.VMEM((rows, units), jnp.bfloat16),
        ],
        compiler_params=pltpu.CompilerParams(vmem_limit_bytes=VMEM_LIMIT),
        cost_estimate=pl.CostEstimate(
            flops=rows * half * units * 24,
            bytes_accessed=half * units * 12 + rows * half * 8,
            transcendentals=rows * units,
        ),
        name="expert_units",
    )(dp_index, modulation, own, left, right, *fars, *weights)


def weigh_kernel(y_ref, ids_ref, dropped_ref, normed_ref, mod_ref, router_ref, weight_ref, rank_ref):
    rows, _ = normed_ref.shape
    hidden_in = (
        normed_ref[...].astype(jnp.float32) * (1.0 + mod_ref[0:1, :]) + mod_ref[1:2, :]
    ).astype(jnp.bfloat16)
    gates = jax.nn.sigmoid(
        lax.dot_general(
            router_ref[...], hidden_in, TRANSPOSED, preferred_element_type=jnp.float32
        )
    )
    which = lax.broadcasted_iota(jnp.int32, gates.shape, 0)
    weights = []
    for offset in OFFSETS:
        expert = lax.rem(y_ref[0] + offset + SIDE, SIDE)
        gate = jnp.sum(jnp.where(which == expert, gates, 0.0), axis=0, keepdims=True)
        kept = jnp.zeros((1, rows), jnp.float32)
        for k in range(2):
            chosen = jnp.where(ids_ref[k : k + 1, :] == expert, 1.0, 0.0)
            kept = kept + chosen * (1.0 - dropped_ref[k : k + 1, :].astype(jnp.float32))
        weights.append(gate * kept)
    weight_ref[...] = jnp.concatenate(weights + weights, axis=0)
    rank_ref[...] = ranks(y_ref, ids_ref)


def weigh(y_index, ids, dropped, normed, modulation, router):
    rows, width = normed.shape
    return pl.pallas_call(
        weigh_kernel,
        out_shape=[jax.ShapeDtypeStruct((8, rows), jnp.float32)] * 2,
        in_specs=[in_smem()] + [in_vmem()] * 5,
        out_specs=[in_vmem()] * 2,
        compiler_params=pltpu.CompilerParams(vmem_limit_bytes=VMEM_LIMIT),
        cost_estimate=pl.CostEstimate(
            flops=2 * 128 * rows * width, bytes_accessed=4 * rows * width, transcendentals=0
        ),
        name="weigh",
    )(y_index, ids, dropped, normed, modulation, router)


def combine_kernel(counts, weight_ref, rank_ref, total_ref, *refs):
    out_ref = refs[-1]
    rows, width = out_ref.shape
    picks, scales = [], []
    for k in range(len(counts)):
        slots = refs[sum(counts[:k])].shape[1]
        slot = lax.broadcasted_iota(jnp.int32, (slots, rows), 0).astype(jnp.float32)
        pick = jnp.where(slot == rank_ref[k : k + 1, :], 1.0, 0.0)
        scales.append(jnp.sum(pick * weight_ref[k : k + 1, :], axis=1, keepdims=True))
        picks.append(pick.astype(jnp.bfloat16))
    half = width // 2
    tile = half // 2
    for start in range(0, width, tile):
        span = slice(start, start + tile)
        side, column = start // half, slice(start % half, start % half + tile)
        total = total_ref[:, span].astype(jnp.float32)
        first = 0
        for pick, scale, count in zip(picks, scales, counts):
            back = sum(
                ref[side, :, column].astype(jnp.float32) for ref in refs[first : first + count]
            )
            first += count
            total = total + lax.dot_general(
                pick,
                (back * scale).astype(jnp.bfloat16),
                (((0,), (0,)), ((), ())),
                preferred_element_type=jnp.float32,
            )
        out_ref[:, span] = total.astype(out_ref.dtype)


def combine(weight, rank, tokens, backs):
    rows, width = tokens.shape
    counts = [len(group) for group in backs]
    return pl.pallas_call(
        functools.partial(combine_kernel, counts),
        out_shape=jax.ShapeDtypeStruct((rows, width), jnp.bfloat16),
        in_specs=[in_vmem()] * (3 + sum(counts)),
        out_specs=in_vmem(),
        compiler_params=pltpu.CompilerParams(vmem_limit_bytes=VMEM_LIMIT),
        cost_estimate=pl.CostEstimate(
            flops=2 * len(backs) * SLOTS * rows * width,
            bytes_accessed=10 * rows * width,
            transcendentals=0,
        ),
        name="add_terms",
    )(weight, rank, tokens, *sum(backs, []))


def on_device(
    tokens,
    text_states,
    text_lengths,
    mod_weight,
    router_weight,
    gate_weight,
    up_weight,
    down_weight,
    expert_ids,
    dropped,
):
    _, rows, width = tokens.shape
    tokens = tokens[0]
    ids = expert_ids[0].T
    owners = lax.axis_size("expert")
    y_index = (lax.axis_index("expert") // SIDE).astype(jnp.int32).reshape(1)
    dp_index = lax.axis_index("dp").astype(jnp.int32).reshape(1)

    def exchange(value, axis="expert"):
        return lax.all_to_all(value, axis, split_axis=0, concat_axis=0, tiled=True)

    normed, *bins = make_bins(y_index, ids, tokens)
    bins = dict(zip(OFFSETS, bins))

    positions = jnp.arange(text_states.shape[1], dtype=jnp.int32)
    valid = (positions[None, :] < text_lengths[:, None]).astype(jnp.bfloat16)
    pooled = jnp.einsum("it,itc->ic", valid, text_states, preferred_element_type=jnp.float32)
    pooled = (pooled / text_lengths.astype(jnp.float32)[:, None]).astype(jnp.bfloat16)
    partial_value = jnp.dot(pooled, mod_weight, preferred_element_type=jnp.float32)

    tie = lax.optimization_barrier
    left_of, right_of, across_x = along_x(-1), along_x(1), along_x(2)

    def both_ways(value):
        return shift(value, right_of), shift(value, left_of)

    def add_half(value, side, extra):
        halves = [value[0], value[1]]
        halves[side] = halves[side] + extra
        return jnp.stack(halves)

    def total_of(*parts):
        return sum(part.astype(jnp.float32) for part in parts).astype(jnp.bfloat16)

    def run(own, near, far):
        return run_expert(dp_index, modulation, own, *near, far, weights)

    middle = bins[0]
    from_up, from_down = shift(bins[1], along_y(1)), shift(bins[-1], along_y(-1))
    from_up, from_down, partial_value, *middle_near = tie(
        (from_up, from_down, partial_value, *both_ways(middle))
    )

    sides = pack(from_up, from_down)
    near = both_ways(sides)
    swap = [(0, 1), (1, 0)]
    owns = tie((gate_weight.T, up_weight.T, down_weight, from_up))[:3]
    swapped = [lax.ppermute(own, "dp", swap) for own in owns]
    columns = jnp.sum(exchange(partial_value, "seq"), axis=0, keepdims=True)
    columns, outer, *rest = tie((columns, bins[2], *near, *swapped))
    near, swapped = rest[:2], rest[2:]
    weights = [owns[0], swapped[0], owns[1], swapped[1], owns[2], swapped[2]]

    far = shift(near[0][0], right_of), shift(near[1][1], left_of)
    outer = shift(outer, along_y(2))
    modulation = exchange(jnp.broadcast_to(columns, (owners, columns.shape[1]))).reshape(2, width)
    modulation, outer, middle, *far = tie((modulation, outer, middle, *far))

    outer_near, outer_far = both_ways(outer), shift(outer, across_x)
    middle_far = shift(middle, across_x)
    out_sides = run(sides, near, far)
    middle_far, outer_far, *rest = tie((middle_far, outer_far, *outer_near, *out_sides))
    outer_near, out_sides = rest[:2], rest[2:]

    got = shift(out_sides[3][0], left_of), shift(out_sides[3][1], right_of)
    out_outer = run(outer, outer_near, (outer_far,))
    rest = tie((*got, *out_outer))
    got, out_outer = rest[:2], rest[2:]

    sums = (
        shift(add_half(out_sides[1], 0, got[0]), left_of),
        shift(add_half(out_sides[2], 1, got[1]), right_of),
    )
    got = shift(out_outer[3][0], left_of), shift(out_outer[3][1], right_of)
    out_middle = run(middle, middle_near, (middle_far,))
    rest = tie((*sums, *got, *out_middle))
    sums, got, out_middle = rest[:2], rest[2:4], rest[4:]

    outer_sums = (
        shift(add_half(out_outer[1], 0, got[0]), left_of),
        shift(add_half(out_outer[2], 1, got[1]), right_of),
    )
    back = total_of(out_sides[0], *sums)
    backs = {
        1: [shift(back[:, :MOST], along_y(-1))],
        -1: [shift(back[:, MOST:], along_y(1))],
    }
    middle_far = shift(out_middle[3], across_x)
    outer_back = total_of(out_outer[0], *outer_sums)
    to_left, to_right, outer_back = tie((out_middle[1], out_middle[2], outer_back))
    middle_sums = middle_far, shift(to_left, left_of), shift(to_right, right_of)
    weight, rank = weigh(y_index, ids, dropped[0].T, normed, modulation, router_weight.T)
    backs[2] = [shift(outer_back, along_y(2))]
    backs[0] = [out_middle[0], *middle_sums]
    total = combine(weight, rank, tokens, [backs[offset] for offset in OFFSETS])
    return total[None]


def solution(mesh):
    return jax.shard_map(
        on_device,
        mesh=mesh,
        in_specs=(
            P(("dp", "seq"), "expert", None),
            P("dp", None, "seq"),
            P("dp"),
            P("seq", "expert"),
            P(),
            P("dp", "expert"),
            P("dp", "expert"),
            P("expert", "dp"),
            P(("dp", "seq"), "expert", None),
            P(("dp", "seq"), "expert", None),
        ),
        out_specs=P(("dp", "seq"), "expert", None),
        check_vma=False,
    )
```

profile of v0, /device:TPU:6, one launch (start us, length us, event | category | flops | bytes accessed | tf_op | source)
XLA Modules:
  0.0 147.2 jit_solution(16137411461593808606)
XLA Ops:
  0.0 1.2 copy-done.1
  1.2 0.7 copy-done.4
  1.9 1.0 normalise_and_bin.1
  2.9 2.3 %collective-permute-start.2 = (bf16[2,72,1280]{2,1,0:T(8,128)(2,1)S(1)}, bf16[2,72,1280]{2,1,0:T(8,128)(2,1)S(1)}, u32[]{:S(2)}, u32[]{:S(2)}) collective-permute-start(bf16[2,72,1280]{2,1,0:T(8,128)(2,1)S(1)} %get-tuple-element.87.own_ref), channel_id=1, source_target_pairs={{0,1},{1,2},{2,3},{3,0},{4,5},{5,6},{6,7},{7,4},{8,9},{9,10},{10,1... | collective-permute-start | bytes 1105928 | tf_op jit(solution)/shard_map/ppermute | solution.py:32
  5.1 1.4 collective-permute-start
  6.5 1.8 %collective-permute-start.1 = (bf16[2,72,1280]{2,1,0:T(8,128)(2,1)S(1)}, bf16[2,72,1280]{2,1,0:T(8,128)(2,1)S(1)}, u32[]{:S(2)}, u32[]{:S(2)}) collective-permute-start(bf16[2,72,1280]{2,1,0:T(8,128)(2,1)S(1)} %get-tuple-element.71), channel_id=1, source_target_pairs={{0,12},{1,13},{2,14},{3,15},{4,0},{5,1},{6,2},{7,3},{8,4},{9,5},{1... | collective-permute-start | bytes 1105928 | tf_op jit(solution)/shard_map/ppermute | solution.py:32
  8.4 0.7 fusion.10
  9.1 0.7 convert_element_type.31
  10.0 1.2 fusion.7
  11.2 2.1 %collective-permute-done.2.left_ref = bf16[2,72,1280]{2,1,0:T(8,128)(2,1)S(1)} collective-permute-done((bf16[2,72,1280]{2,1,0:T(8,128)(2,1)S(1)}, bf16[2,72,1280]{2,1,0:T(8,128)(2,1)S(1)}, u32[]{:S(2)}, u32[]{:S(2)}) %collective-permute-start.2) | collective-permute-done | bytes 368672 | tf_op jit(solution)/shard_map/ppermute | solution.py:32
  13.3 0.7 copy-done.13
  14.6 0.8 copy-done.15
  15.3 0.7 collective-permute-done.first_ref
  17.1 1.8 %collective-permute-start.4 = (bf16[2,136,1280]{2,1,0:T(8,128)(2,1)S(1)}, bf16[2,136,1280]{2,1,0:T(8,128)(2,1)S(1)}, u32[]{:S(2)}, u32[]{:S(2)}) collective-permute-start(bf16[2,136,1280]{2,1,0:T(8,128)(2,1)S(1)} %pack.1.own_ref), channel_id=1, source_target_pairs={{0,1},{1,2},{2,3},{3,0},{4,5},{5,6},{6,7},{7,4},{8,9},{9,10},{10,1... | collective-permute-start | bytes 2088968 | tf_op jit(solution)/shard_map/ppermute | solution.py:32
  19.2 16.0 %all_to_all.15 = f32[8,1,320]{2,1,0:T(1,128)S(1)} all-to-all(f32[8,1,320]{2,1,0:T(1,128)S(1)} %copy.11), channel_id=1, replica_groups=mesh['dp'=2,'seq'=8,'expert'=16] {'seq'}, dimensions={0} | all-to-all | bytes 20480 | tf_op jit(solution)/shard_map/all_to_all | solution.py:324
  35.3 2.6 %collective-permute-done.5.right_ref = bf16[2,136,1280]{2,1,0:T(8,128)(2,1)} collective-permute-done((bf16[2,136,1280]{2,1,0:T(8,128)(2,1)S(1)}, bf16[2,136,1280]{2,1,0:T(8,128)(2,1)}, u32[]{:S(2)}, u32[]{:S(2)}) %collective-permute-start.5) | collective-permute-done | bytes 696352 | tf_op jit(solution)/shard_map/ppermute | solution.py:32
  37.9 0.8 slice_bitcast_fusion.3
  38.9 2.9 %collective-permute-start.9 = (bf16[2,72,1280]{2,1,0:T(8,128)(2,1)}, bf16[2,72,1280]{2,1,0:T(8,128)(2,1)}, u32[]{:S(2)}, u32[]{:S(2)}) collective-permute-start(bf16[2,72,1280]{2,1,0:T(8,128)(2,1)} %copy-done.17), channel_id=1, source_target_pairs={{0,8},{1,9},{2,10},{3,11},{4,12},{5,13},{6,14},{7,15},{8,0},{9,1},... | collective-permute-start | bytes 1105928 | tf_op jit(solution)/shard_map/ppermute | solution.py:32
  41.9 1.8 %slice_bitcast_fusion.2 = bf16[136,1280]{1,0:T(8,128)(2,1)} fusion(bf16[2,136,1280]{2,1,0:T(8,128)(2,1)} %collective-permute-done.5.right_ref), kind=kLoop, calls=%fused_computation.12 | loop fusion | bytes 696320 | tf_op jit(solution)/shard_map/squeeze | solution.py:368
  43.6 1.8 %collective-permute-start.11 = (bf16[136,1280]{1,0:T(8,128)(2,1)}, bf16[136,1280]{1,0:T(8,128)(2,1)}, u32[]{:S(2)}, u32[]{:S(2)}) collective-permute-start(bf16[136,1280]{1,0:T(8,128)(2,1)} %slice_bitcast_fusion.2), channel_id=1, source_target_pairs={{0,3},{1,0},{2,1},{3,2},{4,7},{5,4},{6,5},{7,6},{8,11},{9,8},{10,9... | collective-permute-start | bytes 1044488 | tf_op jit(solution)/shard_map/ppermute | solution.py:32
  46.0 5.3 %all-to-all-start.1 = ((f32[16,1,320]{2,1,0:T(1,128)}), f32[16,1,320]{2,1,0:T(1,128)S(1)}, u32[]{:S(2)}, u32[]{:S(2)}) async-start(f32[16,1,320]{2,1,0:T(1,128)} %broadcast_in_dim.7), calls=%async_computation.1 | async-start | bytes 49152 | tf_op jit(solution)/shard_map/all_to_all | solution.py:324
  51.3 5.6 %all-to-all-done.1 = f32[16,1,320]{2,1,0:T(1,128)S(1)} async-done(((f32[16,1,320]{2,1,0:T(1,128)}), f32[16,1,320]{2,1,0:T(1,128)S(1)}, u32[]{:S(2)}, u32[]{:S(2)}) %all-to-all-start.1) | async-done | bytes 20512 | tf_op jit(solution)/shard_map/all_to_all | solution.py:324
  57.1 2.0 %collective-permute-start.13 = (bf16[2,72,1280]{2,1,0:T(8,128)(2,1)}, bf16[2,72,1280]{2,1,0:T(8,128)(2,1)S(1)}, u32[]{:S(2)}, u32[]{:S(2)}) collective-permute-start(bf16[2,72,1280]{2,1,0:T(8,128)(2,1)} %collective-permute-done.9.own_ref), channel_id=1, source_target_pairs={{0,2},{1,3},{2,0},{3,1},{4,6},{5,7},{6,4},{7,5},{8,10},{9,11},{10,... | collective-permute-start | bytes 1105928 | tf_op jit(solution)/shard_map/ppermute | solution.py:32
  59.1 1.4 collective-permute-start.14
  60.5 0.7 collective-permute-start.15
  61.1 1.6 %collective-permute-start.12 = (bf16[2,72,1280]{2,1,0:T(8,128)(2,1)S(1)}, bf16[2,72,1280]{2,1,0:T(8,128)(2,1)S(1)}, u32[]{:S(2)}, u32[]{:S(2)}) collective-permute-start(bf16[2,72,1280]{2,1,0:T(8,128)(2,1)S(1)} %get-tuple-element.87.own_ref), channel_id=1, source_target_pairs={{0,2},{1,3},{2,0},{3,1},{4,6},{5,7},{6,4},{7,5},{8,10},{9,11},{10,... | collective-permute-start | bytes 1105928 | tf_op jit(solution)/shard_map/ppermute | solution.py:32
  62.8 1.6 %copy-done.7 = bf16[1280,864]{0,1:T(8,128)(2,1)S(1)} copy-done((bf16[1280,864]{0,1:T(8,128)(2,1)S(1)}, bf16[1280,864]{0,1:T(8,128)(2,1)}, u32[]{:S(2)}) %copy-start.7) | copy-done | bytes 2211864
  64.4 1.6 %copy-done.9 = bf16[1280,864]{0,1:T(8,128)(2,1)S(1)} copy-done((bf16[1280,864]{0,1:T(8,128)(2,1)S(1)}, bf16[1280,864]{0,1:T(8,128)(2,1)}, u32[]{:S(2)}) %copy-start.9) | copy-done | bytes 2211864
  66.0 1.6 %copy-done.11 = bf16[864,1280]{1,0:T(8,128)(2,1)S(1)} copy-done((bf16[864,1280]{1,0:T(8,128)(2,1)S(1)}, bf16[864,1280]{1,0:T(8,128)(2,1)}, u32[]{:S(2)}) %copy-start.11) | copy-done | bytes 2211864
  67.6 14.0 %expert_units.3 = (bf16[2,136,1280]{2,1,0:T(8,128)(2,1)S(1)}, bf16[2,136,1280]{2,1,0:T(8,128)(2,1)S(1)}, bf16[2,136,1280]{2,1,0:T(8,128)(2,1)S(1)}, bf16[2,136,1280]{2,1,0:T(8,128)(2,1)S(1)}) custom-call(s32[1]{0:T(128)} %bitcast.15.dp_ref, f32[2,2560]{1,0:T(2,128)S(1)} %reshape.21.mod_ref, bf16[2,136,1280]{2,1,0:T(8,128)(2,1)S(1)} %pack.1.own_ref, ...), custom_call_target="tpu_custom_call" | custom-call | flops 14438891520 | bytes 18841600 | tf_op jit(solution)/shard_map/expert_units/pallas_call | solution.py:197
  81.7 0.8 collective-permute-done.12.refs_0_
  82.5 1.1 collective-permute-start.16
  83.6 2.2 %collective-permute-start.17 = (bf16[136,1280]{1,0:T(8,128)(2,1)S(1)}, bf16[136,1280]{1,0:T(8,128)(2,1)S(1)}, u32[]{:S(2)}, u32[]{:S(2)}) collective-permute-start(bf16[136,1280]{1,0:T(8,128)(2,1)S(1)} %get-tuple-element.135), channel_id=1, source_target_pairs={{0,1},{1,2},{2,3},{3,0},{4,5},{5,6},{6,7},{7,4},{8,9},{9,10},{10,1... | collective-permute-start | bytes 1044488 | tf_op jit(solution)/shard_map/ppermute | solution.py:32
  85.8 9.5 %expert_units.4 = (bf16[2,72,1280]{2,1,0:T(8,128)(2,1)S(1)}, bf16[2,72,1280]{2,1,0:T(8,128)(2,1)S(1)}, bf16[2,72,1280]{2,1,0:T(8,128)(2,1)S(1)}, bf16[2,72,1280]{2,1,0:T(8,128)(2,1)S(1)}) custom-call(s32[1]{0:T(128)} %bitcast.15.dp_ref, f32[2,2560]{1,0:T(2,128)S(1)} %reshape.21.mod_ref, bf16[2,72,1280]{2,1,0:T(8,128)(2,1)} %collective-permute-done.9.own_ref, ...), custom_call_target="tpu_custom_call" | custom-call | flops 7644119040 | bytes 16220160 | tf_op jit(solution)/shard_map/expert_units/pallas_call | solution.py:197
  95.6 0.9 collective-permute-start.19
  96.7 1.3 collective-permute-start.18
  98.1 3.2 %collective-permute-start.21 = (bf16[72,1280]{1,0:T(8,128)(2,1)S(1)}, bf16[72,1280]{1,0:T(8,128)(2,1)S(1)}, u32[]{:S(2)}, u32[]{:S(2)}) collective-permute-start(bf16[72,1280]{1,0:T(8,128)(2,1)S(1)} %get-tuple-element.137), channel_id=1, source_target_pairs={{0,1},{1,2},{2,3},{3,0},{4,5},{5,6},{6,7},{7,4},{8,9},{9,10},{10,1... | collective-permute-start | bytes 552968 | tf_op jit(solution)/shard_map/ppermute | solution.py:32
  101.3 9.4 %expert_units.5 = (bf16[2,72,1280]{2,1,0:T(8,128)(2,1)S(1)}, bf16[2,72,1280]{2,1,0:T(8,128)(2,1)S(1)}, bf16[2,72,1280]{2,1,0:T(8,128)(2,1)S(1)}, bf16[2,72,1280]{2,1,0:T(8,128)(2,1)S(1)}) custom-call(s32[1]{0:T(128)} %bitcast.15.dp_ref, f32[2,2560]{1,0:T(2,128)S(1)} %reshape.21.mod_ref, bf16[2,72,1280]{2,1,0:T(8,128)(2,1)S(1)} %get-tuple-element.87.own_ref, ...), custom_call_target="tpu_custom_call" | custom-call | flops 7644119040 | bytes 16220160 | tf_op jit(solution)/shard_map/expert_units/pallas_call | solution.py:197
  110.7 5.6 %collective-permute-done.20 = bf16[72,1280]{1,0:T(8,128)(2,1)S(1)} collective-permute-done((bf16[72,1280]{1,0:T(8,128)(2,1)S(1)}, bf16[72,1280]{1,0:T(8,128)(2,1)S(1)}, u32[]{:S(2)}, u32[]{:S(2)}) %collective-permute-start.20) | collective-permute-done | bytes 184352 | tf_op jit(solution)/shard_map/ppermute | solution.py:32
  116.4 1.0 collective-permute-start.23
  117.5 2.4 %collective-permute-start.24 = (bf16[2,72,1280]{2,1,0:T(8,128)(2,1)S(1)}, bf16[2,72,1280]{2,1,0:T(8,128)(2,1)S(1)}, u32[]{:S(2)}, u32[]{:S(2)}) collective-permute-start(bf16[2,72,1280]{2,1,0:T(8,128)(2,1)S(1)} %pad_maximum_fusion.3), channel_id=1, source_target_pairs={{0,1},{1,2},{2,3},{3,0},{4,5},{5,6},{6,7},{7,4},{8,9},{9,10},{10,1... | collective-permute-start | bytes 1105928 | tf_op jit(solution)/shard_map/ppermute | solution.py:32
  120.3 1.1 collective-permute-start.27
  121.7 7.2 %collective-permute-done.23 = bf16[2,72,1280]{2,1,0:T(8,128)(2,1)S(1)} collective-permute-done((bf16[2,72,1280]{2,1,0:T(8,128)(2,1)S(1)}, bf16[2,72,1280]{2,1,0:T(8,128)(2,1)S(1)}, u32[]{:S(2)}, u32[]{:S(2)}) %collective-permute-start.23) | collective-permute-done | bytes 368672 | tf_op jit(solution)/shard_map/ppermute | solution.py:32
  129.1 2.2 %collective-permute-start.25 = (bf16[2,72,1280]{2,1,0:T(8,128)(2,1)S(1)}, bf16[2,72,1280]{2,1,0:T(8,128)(2,1)S(1)}, u32[]{:S(2)}, u32[]{:S(2)}) collective-permute-start(bf16[2,72,1280]{2,1,0:T(8,128)(2,1)S(1)} %get-tuple-element.127), channel_id=1, source_target_pairs={{0,3},{1,0},{2,1},{3,2},{4,7},{5,4},{6,5},{7,6},{8,11},{9,8},{10,9... | collective-permute-start | bytes 1105928 | tf_op jit(solution)/shard_map/ppermute | solution.py:32
  131.3 1.1 collective-permute-start.26
  132.4 1.8 %collective-permute-start.29 = (bf16[2,72,1280]{2,1,0:T(8,128)(2,1)S(1)}, bf16[2,72,1280]{2,1,0:T(8,128)(2,1)S(1)}, u32[]{:S(2)}, u32[]{:S(2)}) collective-permute-start(bf16[2,72,1280]{2,1,0:T(8,128)(2,1)S(1)} %add_convert_fusion.1), channel_id=1, source_target_pairs={{0,8},{1,9},{2,10},{3,11},{4,12},{5,13},{6,14},{7,15},{8,0},{9,1},... | collective-permute-start | bytes 1105928 | tf_op jit(solution)/shard_map/ppermute | solution.py:32
  134.6 10.8 %collective-permute-done.28.refs_5_ = bf16[2,68,1280]{2,1,0:T(8,128)(2,1)S(1)} collective-permute-done((bf16[2,68,1280]{2,1,0:T(8,128)(2,1)S(1)}, bf16[2,68,1280]{2,1,0:T(8,128)(2,1)S(1)}, u32[]{:S(2)}, u32[]{:S(2)}) %collective-permute-start.28) | collective-permute-done | bytes 348192 | tf_op jit(solution)/shard_map/ppermute | solution.py:32
  145.4 1.8 %add_terms.1 = bf16[128,2560]{1,0:T(8,128)(2,1)} custom-call(f32[8,128]{1,0:T(8,128)S(1)} %get-tuple-element.85.weight_ref, f32[8,128]{1,0:T(8,128)S(1)} %get-tuple-element.86.rank_ref, bf16[128,2560]{1,0:T(8,128)(2,1)S(1)} %bitcast.60, bf16[2,72,1280]{2,1,0:T(8,128)(2,1)S(1)} %get-tuple-element.118.refs_0_, ...), custom_call_target="tpu_custom_call" | custom-call | flops 188743680 | bytes 3276800 | tf_op jit(solution)/shard_map/add_terms/pallas_call | solution.py:289
  (88 shorter events, 5.2 us)
Async XLA Ops:
  0.0 9.8 %copy-start = (bf16[8,128,512]{2,1,0:T(8,128)(2,1)S(1)}, bf16[8,128,512]{2,1,0:T(8,128)(2,1)}, u32[]{:S(2)}) copy-start(bf16[8,128,512]{2,1,0:T(8,128)(2,1)} %param.11) | copy-start | bytes 3145732
  0.0 1.2 copy-start.1
  2.8 14.2 %copy-start.17 = (bf16[2,72,1280]{2,1,0:T(8,128)(2,1)}, bf16[2,72,1280]{2,1,0:T(8,128)(2,1)S(1)}, u32[]{:S(2)}) copy-start(bf16[2,72,1280]{2,1,0:T(8,128)(2,1)S(1)} %get-tuple-element.81) | copy-start | bytes 1105924
  2.9 10.4 %collective-permute-start.2 = (bf16[2,72,1280]{2,1,0:T(8,128)(2,1)S(1)}, bf16[2,72,1280]{2,1,0:T(8,128)(2,1)S(1)}, u32[]{:S(2)}, u32[]{:S(2)}) collective-permute-start(bf16[2,72,1280]{2,1,0:T(8,128)(2,1)S(1)} %get-tuple-element.87.own_ref), channel_id=1, source_target_pairs={{0,1},{1,2},{2,3},{3,0},{4,5},{5,6},{6,7},{7,4},{8,9},{9,10},{10,1... | collective-permute-start | bytes 1105928 | tf_op jit(solution)/shard_map/ppermute | solution.py:32
  5.1 9.4 %collective-permute-start.3 = (bf16[2,72,1280]{2,1,0:T(8,128)(2,1)S(1)}, bf16[2,72,1280]{2,1,0:T(8,128)(2,1)S(1)}, u32[]{:S(2)}, u32[]{:S(2)}) collective-permute-start(bf16[2,72,1280]{2,1,0:T(8,128)(2,1)S(1)} %get-tuple-element.87.own_ref), channel_id=1, source_target_pairs={{0,3},{1,0},{2,1},{3,2},{4,7},{5,4},{6,5},{7,6},{8,11},{9,8},{10,9... | collective-permute-start | bytes 1105928 | tf_op jit(solution)/shard_map/ppermute | solution.py:32
  5.1 10.8 %collective-permute-start = (bf16[2,72,1280]{2,1,0:T(8,128)(2,1)S(1)}, bf16[2,72,1280]{2,1,0:T(8,128)(2,1)S(1)}, u32[]{:S(2)}, u32[]{:S(2)}) collective-permute-start(bf16[2,72,1280]{2,1,0:T(8,128)(2,1)S(1)} %get-tuple-element.70), channel_id=1, source_target_pairs={{0,4},{1,5},{2,6},{3,7},{4,8},{5,9},{6,10},{7,11},{8,12},{9,13},{1... | collective-permute-start | bytes 1105928 | tf_op jit(solution)/shard_map/ppermute | solution.py:32
  6.5 9.5 %collective-permute-start.1 = (bf16[2,72,1280]{2,1,0:T(8,128)(2,1)S(1)}, bf16[2,72,1280]{2,1,0:T(8,128)(2,1)S(1)}, u32[]{:S(2)}, u32[]{:S(2)}) collective-permute-start(bf16[2,72,1280]{2,1,0:T(8,128)(2,1)S(1)} %get-tuple-element.71), channel_id=1, source_target_pairs={{0,12},{1,13},{2,14},{3,15},{4,0},{5,1},{6,2},{7,3},{8,4},{9,5},{1... | collective-permute-start | bytes 1105928 | tf_op jit(solution)/shard_map/ppermute | solution.py:32
  13.3 0.7 copy-start.13
  14.6 0.8 copy-start.15
  16.0 21.9 %collective-permute-start.6 = (bf16[864,1280]{1,0:T(8,128)(2,1)}, bf16[864,1280]{1,0:T(8,128)(2,1)}, u32[]{:S(2)}, u32[]{:S(2)}) collective-permute-start(bf16[864,1280]{1,0:T(8,128)(2,1)} %bitcast.65), channel_id=1, source_target_pairs={{0,128},{128,0},{1,129},{129,1},{2,130},{130,2},{3,131},{131,3},{4... | collective-permute-start | bytes 6635528 | tf_op jit(solution)/shard_map/ppermute | solution.py:362
  16.0 21.9 %collective-permute-start.7 = (bf16[864,1280]{1,0:T(8,128)(2,1)}, bf16[864,1280]{1,0:T(8,128)(2,1)}, u32[]{:S(2)}, u32[]{:S(2)}) collective-permute-start(bf16[864,1280]{1,0:T(8,128)(2,1)} %bitcast.69), channel_id=1, source_target_pairs={{0,128},{128,0},{1,129},{129,1},{2,130},{130,2},{3,131},{131,3},{4... | collective-permute-start | bytes 6635528 | tf_op jit(solution)/shard_map/ppermute | solution.py:362
  16.5 21.4 %collective-permute-start.8 = (bf16[864,1280]{1,0:T(8,128)(2,1)}, bf16[864,1280]{1,0:T(8,128)(2,1)}, u32[]{:S(2)}, u32[]{:S(2)}) collective-permute-start(bf16[864,1280]{1,0:T(8,128)(2,1)} %refs_5_.1), channel_id=1, source_target_pairs={{0,128},{128,0},{1,129},{129,1},{2,130},{130,2},{3,131},{131,3},{4... | collective-permute-start | bytes 6635528 | tf_op jit(solution)/shard_map/ppermute | solution.py:362
  17.1 18.2 %collective-permute-start.4 = (bf16[2,136,1280]{2,1,0:T(8,128)(2,1)S(1)}, bf16[2,136,1280]{2,1,0:T(8,128)(2,1)S(1)}, u32[]{:S(2)}, u32[]{:S(2)}) collective-permute-start(bf16[2,136,1280]{2,1,0:T(8,128)(2,1)S(1)} %pack.1.own_ref), channel_id=1, source_target_pairs={{0,1},{1,2},{2,3},{3,0},{4,5},{5,6},{6,7},{7,4},{8,9},{9,10},{10,1... | collective-permute-start | bytes 2088968 | tf_op jit(solution)/shard_map/ppermute | solution.py:32
  18.8 19.1 %collective-permute-start.5 = (bf16[2,136,1280]{2,1,0:T(8,128)(2,1)S(1)}, bf16[2,136,1280]{2,1,0:T(8,128)(2,1)}, u32[]{:S(2)}, u32[]{:S(2)}) collective-permute-start(bf16[2,136,1280]{2,1,0:T(8,128)(2,1)S(1)} %pack.1.own_ref), channel_id=1, source_target_pairs={{0,3},{1,0},{2,1},{3,2},{4,7},{5,4},{6,5},{7,6},{8,11},{9,8},{10,9... | collective-permute-start | bytes 2088968 | tf_op jit(solution)/shard_map/ppermute | solution.py:32
  38.7 18.4 %collective-permute-start.10 = (bf16[136,1280]{1,0:T(8,128)(2,1)}, bf16[136,1280]{1,0:T(8,128)(2,1)}, u32[]{:S(2)}, u32[]{:S(2)}) collective-permute-start(bf16[136,1280]{1,0:T(8,128)(2,1)} %slice_bitcast_fusion.3), channel_id=1, source_target_pairs={{0,1},{1,2},{2,3},{3,0},{4,5},{5,6},{6,7},{7,4},{8,9},{9,10},{10,1... | collective-permute-start | bytes 1044488 | tf_op jit(solution)/shard_map/ppermute | solution.py:32
  38.9 18.2 %collective-permute-start.9 = (bf16[2,72,1280]{2,1,0:T(8,128)(2,1)}, bf16[2,72,1280]{2,1,0:T(8,128)(2,1)}, u32[]{:S(2)}, u32[]{:S(2)}) collective-permute-start(bf16[2,72,1280]{2,1,0:T(8,128)(2,1)} %copy-done.17), channel_id=1, source_target_pairs={{0,8},{1,9},{2,10},{3,11},{4,12},{5,13},{6,14},{7,15},{8,0},{9,1},... | collective-permute-start | bytes 1105928 | tf_op jit(solution)/shard_map/ppermute | solution.py:32
  43.6 13.5 %collective-permute-start.11 = (bf16[136,1280]{1,0:T(8,128)(2,1)}, bf16[136,1280]{1,0:T(8,128)(2,1)}, u32[]{:S(2)}, u32[]{:S(2)}) collective-permute-start(bf16[136,1280]{1,0:T(8,128)(2,1)} %slice_bitcast_fusion.2), channel_id=1, source_target_pairs={{0,3},{1,0},{2,1},{3,2},{4,7},{5,4},{6,5},{7,6},{8,11},{9,8},{10,9... | collective-permute-start | bytes 1044488 | tf_op jit(solution)/shard_map/ppermute | solution.py:32
  46.0 11.0 %all-to-all-start.1 = ((f32[16,1,320]{2,1,0:T(1,128)}), f32[16,1,320]{2,1,0:T(1,128)S(1)}, u32[]{:S(2)}, u32[]{:S(2)}) async-start(f32[16,1,320]{2,1,0:T(1,128)} %broadcast_in_dim.7), calls=%async_computation.1 | async-start | bytes 49152 | tf_op jit(solution)/shard_map/all_to_all | solution.py:324
  57.1 25.3 %collective-permute-start.13 = (bf16[2,72,1280]{2,1,0:T(8,128)(2,1)}, bf16[2,72,1280]{2,1,0:T(8,128)(2,1)S(1)}, u32[]{:S(2)}, u32[]{:S(2)}) collective-permute-start(bf16[2,72,1280]{2,1,0:T(8,128)(2,1)} %collective-permute-done.9.own_ref), channel_id=1, source_target_pairs={{0,2},{1,3},{2,0},{3,1},{4,6},{5,7},{6,4},{7,5},{8,10},{9,11},{10,... | collective-permute-start | bytes 1105928 | tf_op jit(solution)/shard_map/ppermute | solution.py:32
  59.1 23.3 %collective-permute-start.14 = (bf16[2,72,1280]{2,1,0:T(8,128)(2,1)}, bf16[2,72,1280]{2,1,0:T(8,128)(2,1)S(1)}, u32[]{:S(2)}, u32[]{:S(2)}) collective-permute-start(bf16[2,72,1280]{2,1,0:T(8,128)(2,1)} %collective-permute-done.9.own_ref), channel_id=1, source_target_pairs={{0,1},{1,2},{2,3},{3,0},{4,5},{5,6},{6,7},{7,4},{8,9},{9,10},{10,1... | collective-permute-start | bytes 1105928 | tf_op jit(solution)/shard_map/ppermute | solution.py:32
  60.5 22.0 %collective-permute-start.15 = (bf16[2,72,1280]{2,1,0:T(8,128)(2,1)}, bf16[2,72,1280]{2,1,0:T(8,128)(2,1)S(1)}, u32[]{:S(2)}, u32[]{:S(2)}) collective-permute-start(bf16[2,72,1280]{2,1,0:T(8,128)(2,1)} %collective-permute-done.9.own_ref), channel_id=1, source_target_pairs={{0,3},{1,0},{2,1},{3,2},{4,7},{5,4},{6,5},{7,6},{8,11},{9,8},{10,9... | collective-permute-start | bytes 1105928 | tf_op jit(solution)/shard_map/ppermute | solution.py:32
  61.1 21.3 %collective-permute-start.12 = (bf16[2,72,1280]{2,1,0:T(8,128)(2,1)S(1)}, bf16[2,72,1280]{2,1,0:T(8,128)(2,1)S(1)}, u32[]{:S(2)}, u32[]{:S(2)}) collective-permute-start(bf16[2,72,1280]{2,1,0:T(8,128)(2,1)S(1)} %get-tuple-element.87.own_ref), channel_id=1, source_target_pairs={{0,2},{1,3},{2,0},{3,1},{4,6},{5,7},{6,4},{7,5},{8,10},{9,11},{10,... | collective-permute-start | bytes 1105928 | tf_op jit(solution)/shard_map/ppermute | solution.py:32
  62.8 1.6 %copy-start.7 = (bf16[1280,864]{0,1:T(8,128)(2,1)S(1)}, bf16[1280,864]{0,1:T(8,128)(2,1)}, u32[]{:S(2)}) copy-start(bf16[1280,864]{0,1:T(8,128)(2,1)} %param.15) | copy-start | bytes 6635524
  64.4 1.6 %copy-start.9 = (bf16[1280,864]{0,1:T(8,128)(2,1)S(1)}, bf16[1280,864]{0,1:T(8,128)(2,1)}, u32[]{:S(2)}) copy-start(bf16[1280,864]{0,1:T(8,128)(2,1)} %param.16) | copy-start | bytes 6635524
  66.0 1.6 %copy-start.11 = (bf16[864,1280]{1,0:T(8,128)(2,1)S(1)}, bf16[864,1280]{1,0:T(8,128)(2,1)}, u32[]{:S(2)}) copy-start(bf16[864,1280]{1,0:T(8,128)(2,1)} %refs_5_.1) | copy-start | bytes 6635524
  82.5 12.9 %collective-permute-start.16 = (bf16[136,1280]{1,0:T(8,128)(2,1)S(1)}, bf16[136,1280]{1,0:T(8,128)(2,1)S(1)}, u32[]{:S(2)}, u32[]{:S(2)}) collective-permute-start(bf16[136,1280]{1,0:T(8,128)(2,1)S(1)} %get-tuple-element.136), channel_id=1, source_target_pairs={{0,3},{1,0},{2,1},{3,2},{4,7},{5,4},{6,5},{7,6},{8,11},{9,8},{10,9... | collective-permute-start | bytes 1044488 | tf_op jit(solution)/shard_map/ppermute | solution.py:32
  83.6 11.8 %collective-permute-start.17 = (bf16[136,1280]{1,0:T(8,128)(2,1)S(1)}, bf16[136,1280]{1,0:T(8,128)(2,1)S(1)}, u32[]{:S(2)}, u32[]{:S(2)}) collective-permute-start(bf16[136,1280]{1,0:T(8,128)(2,1)S(1)} %get-tuple-element.135), channel_id=1, source_target_pairs={{0,1},{1,2},{2,3},{3,0},{4,5},{5,6},{6,7},{7,4},{8,9},{9,10},{10,1... | collective-permute-start | bytes 1044488 | tf_op jit(solution)/shard_map/ppermute | solution.py:32
  85.8 15.5 %copy-start.16 = (bf16[2,72,1280]{2,1,0:T(8,128)(2,1)S(1)}, bf16[2,72,1280]{2,1,0:T(8,128)(2,1)}, u32[]{:S(2)}) copy-start(bf16[2,72,1280]{2,1,0:T(8,128)(2,1)} %copy-done.15) | copy-start | bytes 1105924
  95.4 5.9 %copy-start.12 = (bf16[864,1280]{1,0:T(8,128)(2,1)S(1)}, bf16[864,1280]{1,0:T(8,128)(2,1)}, u32[]{:S(2)}) copy-start(bf16[864,1280]{1,0:T(8,128)(2,1)} %refs_5_.1) | copy-start | bytes 6635524
  95.5 5.8 %copy-start.14 = (bf16[2,72,1280]{2,1,0:T(8,128)(2,1)S(1)}, bf16[2,72,1280]{2,1,0:T(8,128)(2,1)}, u32[]{:S(2)}) copy-start(bf16[2,72,1280]{2,1,0:T(8,128)(2,1)} %copy-done.13) | copy-start | bytes 1105924
  95.6 5.8 %copy-start.8 = (bf16[1280,864]{0,1:T(8,128)(2,1)S(1)}, bf16[1280,864]{0,1:T(8,128)(2,1)}, u32[]{:S(2)}) copy-start(bf16[1280,864]{0,1:T(8,128)(2,1)} %param.15) | copy-start | bytes 6635524
  95.6 5.8 %copy-start.10 = (bf16[1280,864]{0,1:T(8,128)(2,1)S(1)}, bf16[1280,864]{0,1:T(8,128)(2,1)}, u32[]{:S(2)}) copy-start(bf16[1280,864]{0,1:T(8,128)(2,1)} %param.16) | copy-start | bytes 6635524
  95.6 20.7 %collective-permute-start.19 = (bf16[2,136,1280]{2,1,0:T(8,128)(2,1)S(1)}, bf16[2,136,1280]{2,1,0:T(8,128)(2,1)S(1)}, u32[]{:S(2)}, u32[]{:S(2)}) collective-permute-start(bf16[2,136,1280]{2,1,0:T(8,128)(2,1)S(1)} %pad_maximum_fusion.1), channel_id=1, source_target_pairs={{0,1},{1,2},{2,3},{3,0},{4,5},{5,6},{6,7},{7,4},{8,9},{9,10},{10,1... | collective-permute-start | bytes 2088968 | tf_op jit(solution)/shard_map/ppermute | solution.py:32
  96.7 19.6 %collective-permute-start.18 = (bf16[2,136,1280]{2,1,0:T(8,128)(2,1)S(1)}, bf16[2,136,1280]{2,1,0:T(8,128)(2,1)S(1)}, u32[]{:S(2)}, u32[]{:S(2)}) collective-permute-start(bf16[2,136,1280]{2,1,0:T(8,128)(2,1)S(1)} %pad_maximum_fusion), channel_id=1, source_target_pairs={{0,3},{1,0},{2,1},{3,2},{4,7},{5,4},{6,5},{7,6},{8,11},{9,8},{10,9... | collective-permute-start | bytes 2088968 | tf_op jit(solution)/shard_map/ppermute | solution.py:32
  98.0 18.3 %collective-permute-start.20 = (bf16[72,1280]{1,0:T(8,128)(2,1)S(1)}, bf16[72,1280]{1,0:T(8,128)(2,1)S(1)}, u32[]{:S(2)}, u32[]{:S(2)}) collective-permute-start(bf16[72,1280]{1,0:T(8,128)(2,1)S(1)} %get-tuple-element.138), channel_id=1, source_target_pairs={{0,3},{1,0},{2,1},{3,2},{4,7},{5,4},{6,5},{7,6},{8,11},{9,8},{10,9... | collective-permute-start | bytes 552968 | tf_op jit(solution)/shard_map/ppermute | solution.py:32
  98.1 18.2 %collective-permute-start.21 = (bf16[72,1280]{1,0:T(8,128)(2,1)S(1)}, bf16[72,1280]{1,0:T(8,128)(2,1)S(1)}, u32[]{:S(2)}, u32[]{:S(2)}) collective-permute-start(bf16[72,1280]{1,0:T(8,128)(2,1)S(1)} %get-tuple-element.137), channel_id=1, source_target_pairs={{0,1},{1,2},{2,3},{3,0},{4,5},{5,6},{6,7},{7,4},{8,9},{9,10},{10,1... | collective-permute-start | bytes 552968 | tf_op jit(solution)/shard_map/ppermute | solution.py:32
  116.4 12.5 %collective-permute-start.23 = (bf16[2,72,1280]{2,1,0:T(8,128)(2,1)S(1)}, bf16[2,72,1280]{2,1,0:T(8,128)(2,1)S(1)}, u32[]{:S(2)}, u32[]{:S(2)}) collective-permute-start(bf16[2,72,1280]{2,1,0:T(8,128)(2,1)S(1)} %pad_maximum_fusion.2), channel_id=1, source_target_pairs={{0,3},{1,0},{2,1},{3,2},{4,7},{5,4},{6,5},{7,6},{8,11},{9,8},{10,9... | collective-permute-start | bytes 1105928 | tf_op jit(solution)/shard_map/ppermute | solution.py:32
  117.5 16.7 %copy-start.3 = (bf16[2560,4]{0,1:T(4,128)(2,1)S(1)}, bf16[2560,4]{0,1:T(4,128)(2,1)}, u32[]{:S(2)}) copy-start(bf16[2560,4]{0,1:T(4,128)(2,1)} %param.14) | copy-start | bytes 61444
  117.5 16.7 %copy-start.5 = (s32[1,128,2]{1,2,0:T(2,128)S(1)}, s32[1,128,2]{1,2,0:T(2,128)}, u32[]{:S(2)}) copy-start(s32[1,128,2]{1,2,0:T(2,128)} %param.18) | copy-start | bytes 3076
  117.5 16.7 %copy-start.6 = (s32[1,128,2]{1,2,0:T(2,128)S(1)}, s32[1,128,2]{1,2,0:T(2,128)}, u32[]{:S(2)}) copy-start(s32[1,128,2]{1,2,0:T(2,128)} %param.19) | copy-start | bytes 3076
  117.5 11.4 %collective-permute-start.24 = (bf16[2,72,1280]{2,1,0:T(8,128)(2,1)S(1)}, bf16[2,72,1280]{2,1,0:T(8,128)(2,1)S(1)}, u32[]{:S(2)}, u32[]{:S(2)}) collective-permute-start(bf16[2,72,1280]{2,1,0:T(8,128)(2,1)S(1)} %pad_maximum_fusion.3), channel_id=1, source_target_pairs={{0,1},{1,2},{2,3},{3,0},{4,5},{5,6},{6,7},{7,4},{8,9},{9,10},{10,1... | collective-permute-start | bytes 1105928 | tf_op jit(solution)/shard_map/ppermute | solution.py:32
  120.2 25.2 %copy-start.2 = (bf16[1,128,2560]{2,1,0:T(8,128)(2,1)S(1)}, bf16[1,128,2560]{2,1,0:T(8,128)(2,1)}, u32[]{:S(2)}) copy-start(bf16[1,128,2560]{2,1,0:T(8,128)(2,1)} %param.10) | copy-start | bytes 1966084
  120.3 14.0 %collective-permute-start.27 = (bf16[2,68,1280]{2,1,0:T(8,128)(2,1)S(1)}, bf16[2,68,1280]{2,1,0:T(8,128)(2,1)S(1)}, u32[]{:S(2)}, u32[]{:S(2)}) collective-permute-start(bf16[2,68,1280]{2,1,0:T(8,128)(2,1)S(1)} %get-tuple-element.134), channel_id=1, source_target_pairs={{0,12},{1,13},{2,14},{3,15},{4,0},{5,1},{6,2},{7,3},{8,4},{9,5},{1... | collective-permute-start | bytes 1044488 | tf_op jit(solution)/shard_map/ppermute | solution.py:32
  121.4 24.0 %collective-permute-start.22 = (bf16[2,72,1280]{2,1,0:T(8,128)(2,1)S(1)}, bf16[2,72,1280]{2,1,0:T(8,128)(2,1)S(1)}, u32[]{:S(2)}, u32[]{:S(2)}) collective-permute-start(bf16[2,72,1280]{2,1,0:T(8,128)(2,1)S(1)} %get-tuple-element.119), channel_id=1, source_target_pairs={{0,2},{1,3},{2,0},{3,1},{4,6},{5,7},{6,4},{7,5},{8,10},{9,11},{10,... | collective-permute-start | bytes 1105928 | tf_op jit(solution)/shard_map/ppermute | solution.py:32
  129.1 16.3 %collective-permute-start.25 = (bf16[2,72,1280]{2,1,0:T(8,128)(2,1)S(1)}, bf16[2,72,1280]{2,1,0:T(8,128)(2,1)S(1)}, u32[]{:S(2)}, u32[]{:S(2)}) collective-permute-start(bf16[2,72,1280]{2,1,0:T(8,128)(2,1)S(1)} %get-tuple-element.127), channel_id=1, source_target_pairs={{0,3},{1,0},{2,1},{3,2},{4,7},{5,4},{6,5},{7,6},{8,11},{9,8},{10,9... | collective-permute-start | bytes 1105928 | tf_op jit(solution)/shard_map/ppermute | solution.py:32
  131.3 14.1 %collective-permute-start.26 = (bf16[2,72,1280]{2,1,0:T(8,128)(2,1)S(1)}, bf16[2,72,1280]{2,1,0:T(8,128)(2,1)S(1)}, u32[]{:S(2)}, u32[]{:S(2)}) collective-permute-start(bf16[2,72,1280]{2,1,0:T(8,128)(2,1)S(1)} %get-tuple-element.128), channel_id=1, source_target_pairs={{0,1},{1,2},{2,3},{3,0},{4,5},{5,6},{6,7},{7,4},{8,9},{9,10},{10,1... | collective-permute-start | bytes 1105928 | tf_op jit(solution)/shard_map/ppermute | solution.py:32
  132.4 13.0 %collective-permute-start.29 = (bf16[2,72,1280]{2,1,0:T(8,128)(2,1)S(1)}, bf16[2,72,1280]{2,1,0:T(8,128)(2,1)S(1)}, u32[]{:S(2)}, u32[]{:S(2)}) collective-permute-start(bf16[2,72,1280]{2,1,0:T(8,128)(2,1)S(1)} %add_convert_fusion.1), channel_id=1, source_target_pairs={{0,8},{1,9},{2,10},{3,11},{4,12},{5,13},{6,14},{7,15},{8,0},{9,1},... | collective-permute-start | bytes 1105928 | tf_op jit(solution)/shard_map/ppermute | solution.py:32
  134.2 11.1 %collective-permute-start.28 = (bf16[2,68,1280]{2,1,0:T(8,128)(2,1)S(1)}, bf16[2,68,1280]{2,1,0:T(8,128)(2,1)S(1)}, u32[]{:S(2)}, u32[]{:S(2)}) collective-permute-start(bf16[2,68,1280]{2,1,0:T(8,128)(2,1)S(1)} %get-tuple-element.133), channel_id=1, source_target_pairs={{0,4},{1,5},{2,6},{3,7},{4,8},{5,9},{6,10},{7,11},{8,12},{9,13},{1... | collective-permute-start | bytes 1044488 | tf_op jit(solution)/shard_map/ppermute | solution.py:32
  (1 other events, 0.7 us)
where the time goes:
time: 150 us; the launch traced here: 147 us
  starting transfers between devices  42.8 us (29%)
  Pallas kernels  36.5 us (24%)
  waiting for transfers between devices  36 us (24%)
  blocking collectives  16 us (11%)
  local copies, waits for them, and re-layouts  11.8 us (8%)
  other arithmetic  2.27 us (2%)
    ppermute x27, starting transfers between devices, shift(): return lax.ppermute(value, 'expert', perm)  37 us
    pallas_call x3, Pallas kernels, run_expert(): pl.pallas_call(expert_kernel, out_shape=[jax.ShapeDtypeStruct(own.shape,...  32.9 us
    ppermute x27, waiting for transfers between devices, shift(): return lax.ppermute(value, 'expert', perm)  30.3 us
    all_to_all x1, blocking collectives, exchange(): return lax.all_to_all(value, axis, split_axis=0, concat_axis=0, tiled=True)  16 us
    unnamed x36, local copies, waits for them, and re-layouts  8.3 us
    all_to_all x1, waiting for transfers between devices, exchange(): return lax.all_to_all(value, axis, split_axis=0, concat_axis=0, tiled=True)  5.64 us
    all_to_all x1, starting transfers between devices, exchange(): return lax.all_to_all(value, axis, split_axis=0, concat_axis=0, tiled=True)  5.31 us
  transfers between devices with their start and end apart: 31, of which 9 were waited for; matrix products, arithmetic and copies ran while one was open for 4% of the time, Pallas kernels for 23%

commit v1 on v0

--- a/solution.py
+++ b/solution.py
@@ -401,7 +401,10 @@
     }
     middle_far = shift(out_middle[3], across_x)
     outer_back = total_of(out_outer[0], *outer_sums)
-    to_left, to_right, outer_back = tie((out_middle[1], out_middle[2], outer_back))
+    to_left, to_right, outer_back, *sides_back = tie(
+        (out_middle[1], out_middle[2], outer_back, backs[1][0], backs[-1][0])
+    )
+    backs = {1: sides_back[:1], -1: sides_back[1:]}
     middle_sums = middle_far, shift(to_left, left_of), shift(to_right, right_of)
     weight, rank = weigh(y_index, ids, dropped[0].T, normed, modulation, router_weight.T)
     backs[2] = [shift(outer_back, along_y(2))]

time: 150 us -> 149 us (level); the launches traced: 147 us -> 148 us
  waiting for transfers between devices: 36 us -> 38.1 us
    ppermute x27, waiting for transfers between devices: 30.3 us -> 32.5 us  [shift(): return lax.ppermute(value, 'expert', perm)]
  transfers between devices with their start and end apart: 31 -> 31, of which waited for: 9 -> 11; matrix products, arithmetic and copies ran while one was open for 4% -> 4% of each run, Pallas kernels for 23% -> 23%
where the time goes in v1:
time: 149 us; the launch traced here: 148 us
  starting transfers between devices  41.6 us (28%)
  waiting for transfers between devices  38.1 us (26%)
  Pallas kernels  36.5 us (24%)
  blocking collectives  16 us (11%)
  local copies, waits for them, and re-layouts  11.8 us (8%)
  other arithmetic  2.27 us (2%)
    ppermute x27, starting transfers between devices, shift(): return lax.ppermute(value, 'expert', perm)  35.8 us
    pallas_call x3, Pallas kernels, run_expert(): pl.pallas_call(expert_kernel, out_shape=[jax.ShapeDtypeStruct(own.shape,...  32.9 us
    ppermute x27, waiting for transfers between devices, shift(): return lax.ppermute(value, 'expert', perm)  32.5 us
    all_to_all x1, blocking collectives, exchange(): return lax.all_to_all(value, axis, split_axis=0, concat_axis=0, tiled=True)  16 us
    unnamed x36, local copies, waits for them, and re-layouts  8.3 us
    all_to_all x1, waiting for transfers between devices, exchange(): return lax.all_to_all(value, axis, split_axis=0, concat_axis=0, tiled=True)  5.64 us
    all_to_all x1, starting transfers between devices, exchange(): return lax.all_to_all(value, axis, split_axis=0, concat_axis=0, tiled=True)  5.31 us
  transfers between devices with their start and end apart: 31, of which 11 were waited for; matrix products, arithmetic and copies ran while one was open for 4% of the time, Pallas kernels for 23%

profile of v1, /device:TPU:6, one launch (start us, length us, event | category | flops | bytes accessed | tf_op | source)
XLA Modules:
  0.0 148.1 jit_solution(14531317197634595334)
XLA Ops:
  0.0 1.2 copy-done.1
  1.2 0.7 copy-done.4
  1.9 1.0 normalise_and_bin.1
  2.9 2.3 %collective-permute-start.2 = (bf16[2,72,1280]{2,1,0:T(8,128)(2,1)S(1)}, bf16[2,72,1280]{2,1,0:T(8,128)(2,1)S(1)}, u32[]{:S(2)}, u32[]{:S(2)}) collective-permute-start(bf16[2,72,1280]{2,1,0:T(8,128)(2,1)S(1)} %get-tuple-element.89.own_ref), channel_id=1, source_target_pairs={{0,1},{1,2},{2,3},{3,0},{4,5},{5,6},{6,7},{7,4},{8,9},{9,10},{10,1... | collective-permute-start | bytes 1105928 | tf_op jit(solution)/shard_map/ppermute | solution.py:32
  5.1 1.4 collective-permute-start
  6.5 1.8 %collective-permute-start.1 = (bf16[2,72,1280]{2,1,0:T(8,128)(2,1)S(1)}, bf16[2,72,1280]{2,1,0:T(8,128)(2,1)S(1)}, u32[]{:S(2)}, u32[]{:S(2)}) collective-permute-start(bf16[2,72,1280]{2,1,0:T(8,128)(2,1)S(1)} %get-tuple-element.73), channel_id=1, source_target_pairs={{0,12},{1,13},{2,14},{3,15},{4,0},{5,1},{6,2},{7,3},{8,4},{9,5},{1... | collective-permute-start | bytes 1105928 | tf_op jit(solution)/shard_map/ppermute | solution.py:32
  8.4 0.7 fusion.10
  9.1 0.7 convert_element_type.31
  10.0 1.2 fusion.7
  11.2 2.1 %collective-permute-done.2.left_ref = bf16[2,72,1280]{2,1,0:T(8,128)(2,1)S(1)} collective-permute-done((bf16[2,72,1280]{2,1,0:T(8,128)(2,1)S(1)}, bf16[2,72,1280]{2,1,0:T(8,128)(2,1)S(1)}, u32[]{:S(2)}, u32[]{:S(2)}) %collective-permute-start.2) | collective-permute-done | bytes 368672 | tf_op jit(solution)/shard_map/ppermute | solution.py:32
  13.3 0.7 copy-done.13
  14.6 0.8 copy-done.15
  15.3 0.7 collective-permute-done.first_ref
  17.1 1.8 %collective-permute-start.4 = (bf16[2,136,1280]{2,1,0:T(8,128)(2,1)S(1)}, bf16[2,136,1280]{2,1,0:T(8,128)(2,1)S(1)}, u32[]{:S(2)}, u32[]{:S(2)}) collective-permute-start(bf16[2,136,1280]{2,1,0:T(8,128)(2,1)S(1)} %pack.1.own_ref), channel_id=1, source_target_pairs={{0,1},{1,2},{2,3},{3,0},{4,5},{5,6},{6,7},{7,4},{8,9},{9,10},{10,1... | collective-permute-start | bytes 2088968 | tf_op jit(solution)/shard_map/ppermute | solution.py:32
  19.2 16.0 %all_to_all.15 = f32[8,1,320]{2,1,0:T(1,128)S(1)} all-to-all(f32[8,1,320]{2,1,0:T(1,128)S(1)} %copy.11), channel_id=1, replica_groups=mesh['dp'=2,'seq'=8,'expert'=16] {'seq'}, dimensions={0} | all-to-all | bytes 20480 | tf_op jit(solution)/shard_map/all_to_all | solution.py:324
  35.3 2.6 %collective-permute-done.5.right_ref = bf16[2,136,1280]{2,1,0:T(8,128)(2,1)} collective-permute-done((bf16[2,136,1280]{2,1,0:T(8,128)(2,1)S(1)}, bf16[2,136,1280]{2,1,0:T(8,128)(2,1)}, u32[]{:S(2)}, u32[]{:S(2)}) %collective-permute-start.5) | collective-permute-done | bytes 696352 | tf_op jit(solution)/shard_map/ppermute | solution.py:32
  37.9 0.8 slice_bitcast_fusion.3
  38.9 2.9 %collective-permute-start.9 = (bf16[2,72,1280]{2,1,0:T(8,128)(2,1)}, bf16[2,72,1280]{2,1,0:T(8,128)(2,1)}, u32[]{:S(2)}, u32[]{:S(2)}) collective-permute-start(bf16[2,72,1280]{2,1,0:T(8,128)(2,1)} %copy-done.17), channel_id=1, source_target_pairs={{0,8},{1,9},{2,10},{3,11},{4,12},{5,13},{6,14},{7,15},{8,0},{9,1},... | collective-permute-start | bytes 1105928 | tf_op jit(solution)/shard_map/ppermute | solution.py:32
  41.9 1.8 %slice_bitcast_fusion.2 = bf16[136,1280]{1,0:T(8,128)(2,1)} fusion(bf16[2,136,1280]{2,1,0:T(8,128)(2,1)} %collective-permute-done.5.right_ref), kind=kLoop, calls=%fused_computation.12 | loop fusion | bytes 696320 | tf_op jit(solution)/shard_map/squeeze | solution.py:368
  43.6 1.8 %collective-permute-start.11 = (bf16[136,1280]{1,0:T(8,128)(2,1)}, bf16[136,1280]{1,0:T(8,128)(2,1)}, u32[]{:S(2)}, u32[]{:S(2)}) collective-permute-start(bf16[136,1280]{1,0:T(8,128)(2,1)} %slice_bitcast_fusion.2), channel_id=1, source_target_pairs={{0,3},{1,0},{2,1},{3,2},{4,7},{5,4},{6,5},{7,6},{8,11},{9,8},{10,9... | collective-permute-start | bytes 1044488 | tf_op jit(solution)/shard_map/ppermute | solution.py:32
  46.0 5.3 %all-to-all-start.1 = ((f32[16,1,320]{2,1,0:T(1,128)}), f32[16,1,320]{2,1,0:T(1,128)S(1)}, u32[]{:S(2)}, u32[]{:S(2)}) async-start(f32[16,1,320]{2,1,0:T(1,128)} %broadcast_in_dim.7), calls=%async_computation.1 | async-start | bytes 49152 | tf_op jit(solution)/shard_map/all_to_all | solution.py:324
  51.3 5.6 %all-to-all-done.1 = f32[16,1,320]{2,1,0:T(1,128)S(1)} async-done(((f32[16,1,320]{2,1,0:T(1,128)}), f32[16,1,320]{2,1,0:T(1,128)S(1)}, u32[]{:S(2)}, u32[]{:S(2)}) %all-to-all-start.1) | async-done | bytes 20512 | tf_op jit(solution)/shard_map/all_to_all | solution.py:324
  57.1 2.0 %collective-permute-start.13 = (bf16[2,72,1280]{2,1,0:T(8,128)(2,1)}, bf16[2,72,1280]{2,1,0:T(8,128)(2,1)S(1)}, u32[]{:S(2)}, u32[]{:S(2)}) collective-permute-start(bf16[2,72,1280]{2,1,0:T(8,128)(2,1)} %collective-permute-done.9.own_ref), channel_id=1, source_target_pairs={{0,2},{1,3},{2,0},{3,1},{4,6},{5,7},{6,4},{7,5},{8,10},{9,11},{10,... | collective-permute-start | bytes 1105928 | tf_op jit(solution)/shard_map/ppermute | solution.py:32
  59.1 1.4 collective-permute-start.14
  61.1 1.6 %collective-permute-start.12 = (bf16[2,72,1280]{2,1,0:T(8,128)(2,1)S(1)}, bf16[2,72,1280]{2,1,0:T(8,128)(2,1)S(1)}, u32[]{:S(2)}, u32[]{:S(2)}) collective-permute-start(bf16[2,72,1280]{2,1,0:T(8,128)(2,1)S(1)} %get-tuple-element.89.own_ref), channel_id=1, source_target_pairs={{0,2},{1,3},{2,0},{3,1},{4,6},{5,7},{6,4},{7,5},{8,10},{9,11},{10,... | collective-permute-start | bytes 1105928 | tf_op jit(solution)/shard_map/ppermute | solution.py:32
  62.8 1.6 %copy-done.7 = bf16[1280,864]{0,1:T(8,128)(2,1)S(1)} copy-done((bf16[1280,864]{0,1:T(8,128)(2,1)S(1)}, bf16[1280,864]{0,1:T(8,128)(2,1)}, u32[]{:S(2)}) %copy-start.7) | copy-done | bytes 2211864
  64.4 1.6 %copy-done.9 = bf16[1280,864]{0,1:T(8,128)(2,1)S(1)} copy-done((bf16[1280,864]{0,1:T(8,128)(2,1)S(1)}, bf16[1280,864]{0,1:T(8,128)(2,1)}, u32[]{:S(2)}) %copy-start.9) | copy-done | bytes 2211864
  66.0 1.6 %copy-done.11 = bf16[864,1280]{1,0:T(8,128)(2,1)S(1)} copy-done((bf16[864,1280]{1,0:T(8,128)(2,1)S(1)}, bf16[864,1280]{1,0:T(8,128)(2,1)}, u32[]{:S(2)}) %copy-start.11) | copy-done | bytes 2211864
  67.6 14.0 %expert_units.3 = (bf16[2,136,1280]{2,1,0:T(8,128)(2,1)S(1)}, bf16[2,136,1280]{2,1,0:T(8,128)(2,1)S(1)}, bf16[2,136,1280]{2,1,0:T(8,128)(2,1)S(1)}, bf16[2,136,1280]{2,1,0:T(8,128)(2,1)S(1)}) custom-call(s32[1]{0:T(128)} %bitcast.15.dp_ref, f32[2,2560]{1,0:T(2,128)S(1)} %reshape.21.mod_ref, bf16[2,136,1280]{2,1,0:T(8,128)(2,1)S(1)} %pack.1.own_ref, ...), custom_call_target="tpu_custom_call" | custom-call | flops 14438891520 | bytes 18841600 | tf_op jit(solution)/shard_map/expert_units/pallas_call | solution.py:197
  81.7 0.8 collective-permute-done.12.refs_0_
  82.5 1.1 collective-permute-start.16
  83.6 2.2 %collective-permute-start.17 = (bf16[136,1280]{1,0:T(8,128)(2,1)S(1)}, bf16[136,1280]{1,0:T(8,128)(2,1)S(1)}, u32[]{:S(2)}, u32[]{:S(2)}) collective-permute-start(bf16[136,1280]{1,0:T(8,128)(2,1)S(1)} %get-tuple-element.139), channel_id=1, source_target_pairs={{0,1},{1,2},{2,3},{3,0},{4,5},{5,6},{6,7},{7,4},{8,9},{9,10},{10,1... | collective-permute-start | bytes 1044488 | tf_op jit(solution)/shard_map/ppermute | solution.py:32
  85.8 9.5 %expert_units.4 = (bf16[2,72,1280]{2,1,0:T(8,128)(2,1)S(1)}, bf16[2,72,1280]{2,1,0:T(8,128)(2,1)S(1)}, bf16[2,72,1280]{2,1,0:T(8,128)(2,1)S(1)}, bf16[2,72,1280]{2,1,0:T(8,128)(2,1)S(1)}) custom-call(s32[1]{0:T(128)} %bitcast.15.dp_ref, f32[2,2560]{1,0:T(2,128)S(1)} %reshape.21.mod_ref, bf16[2,72,1280]{2,1,0:T(8,128)(2,1)} %collective-permute-done.9.own_ref, ...), custom_call_target="tpu_custom_call" | custom-call | flops 7644119040 | bytes 16220160 | tf_op jit(solution)/shard_map/expert_units/pallas_call | solution.py:197
  95.6 0.9 collective-permute-start.19
  96.7 1.3 collective-permute-start.18
  98.1 3.2 %collective-permute-start.21 = (bf16[72,1280]{1,0:T(8,128)(2,1)S(1)}, bf16[72,1280]{1,0:T(8,128)(2,1)S(1)}, u32[]{:S(2)}, u32[]{:S(2)}) collective-permute-start(bf16[72,1280]{1,0:T(8,128)(2,1)S(1)} %get-tuple-element.141), channel_id=1, source_target_pairs={{0,1},{1,2},{2,3},{3,0},{4,5},{5,6},{6,7},{7,4},{8,9},{9,10},{10,1... | collective-permute-start | bytes 552968 | tf_op jit(solution)/shard_map/ppermute | solution.py:32
  101.3 9.4 %expert_units.5 = (bf16[2,72,1280]{2,1,0:T(8,128)(2,1)S(1)}, bf16[2,72,1280]{2,1,0:T(8,128)(2,1)S(1)}, bf16[2,72,1280]{2,1,0:T(8,128)(2,1)S(1)}, bf16[2,72,1280]{2,1,0:T(8,128)(2,1)S(1)}) custom-call(s32[1]{0:T(128)} %bitcast.15.dp_ref, f32[2,2560]{1,0:T(2,128)S(1)} %reshape.21.mod_ref, bf16[2,72,1280]{2,1,0:T(8,128)(2,1)S(1)} %get-tuple-element.89.own_ref, ...), custom_call_target="tpu_custom_call" | custom-call | flops 7644119040 | bytes 16220160 | tf_op jit(solution)/shard_map/expert_units/pallas_call | solution.py:197
  110.7 5.6 %collective-permute-done.20 = bf16[72,1280]{1,0:T(8,128)(2,1)S(1)} collective-permute-done((bf16[72,1280]{1,0:T(8,128)(2,1)S(1)}, bf16[72,1280]{1,0:T(8,128)(2,1)S(1)}, u32[]{:S(2)}, u32[]{:S(2)}) %collective-permute-start.20) | collective-permute-done | bytes 184352 | tf_op jit(solution)/shard_map/ppermute | solution.py:32
  116.4 1.0 collective-permute-start.23
  117.5 2.4 %collective-permute-start.24 = (bf16[2,72,1280]{2,1,0:T(8,128)(2,1)S(1)}, bf16[2,72,1280]{2,1,0:T(8,128)(2,1)S(1)}, u32[]{:S(2)}, u32[]{:S(2)}) collective-permute-start(bf16[2,72,1280]{2,1,0:T(8,128)(2,1)S(1)} %pad_maximum_fusion.3), channel_id=1, source_target_pairs={{0,1},{1,2},{2,3},{3,0},{4,5},{5,6},{6,7},{7,4},{8,9},{9,10},{10,1... | collective-permute-start | bytes 1105928 | tf_op jit(solution)/shard_map/ppermute | solution.py:32
  120.3 1.1 collective-permute-start.25
  121.4 1.0 collective-permute-start.26
  122.4 8.1 %collective-permute-done.23 = bf16[2,72,1280]{2,1,0:T(8,128)(2,1)S(1)} collective-permute-done((bf16[2,72,1280]{2,1,0:T(8,128)(2,1)S(1)}, bf16[2,72,1280]{2,1,0:T(8,128)(2,1)S(1)}, u32[]{:S(2)}, u32[]{:S(2)}) %collective-permute-start.23) | collective-permute-done | bytes 368672 | tf_op jit(solution)/shard_map/ppermute | solution.py:32
  130.6 3.4 %collective-permute-done.26.refs_5_ = bf16[2,68,1280]{2,1,0:T(8,128)(2,1)S(1)} collective-permute-done((bf16[2,68,1280]{2,1,0:T(8,128)(2,1)S(1)}, bf16[2,68,1280]{2,1,0:T(8,128)(2,1)S(1)}, u32[]{:S(2)}, u32[]{:S(2)}) %collective-permute-start.26) | collective-permute-done | bytes 348192 | tf_op jit(solution)/shard_map/ppermute | solution.py:32
  134.3 2.9 %collective-permute-start.28 = (bf16[2,72,1280]{2,1,0:T(8,128)(2,1)S(1)}, bf16[2,72,1280]{2,1,0:T(8,128)(2,1)S(1)}, u32[]{:S(2)}, u32[]{:S(2)}) collective-permute-start(bf16[2,72,1280]{2,1,0:T(8,128)(2,1)S(1)} %get-tuple-element.133), channel_id=1, source_target_pairs={{0,1},{1,2},{2,3},{3,0},{4,5},{5,6},{6,7},{7,4},{8,9},{9,10},{10,1... | collective-permute-start | bytes 1105928 | tf_op jit(solution)/shard_map/ppermute | solution.py:32
  137.6 5.1 %collective-permute-done.27.refs_2_ = bf16[2,72,1280]{2,1,0:T(8,128)(2,1)S(1)} collective-permute-done((bf16[2,72,1280]{2,1,0:T(8,128)(2,1)S(1)}, bf16[2,72,1280]{2,1,0:T(8,128)(2,1)S(1)}, u32[]{:S(2)}, u32[]{:S(2)}) %collective-permute-start.27) | collective-permute-done | bytes 368672 | tf_op jit(solution)/shard_map/ppermute | solution.py:32
  142.8 3.5 %collective-permute-done.29.refs_6_ = bf16[2,72,1280]{2,1,0:T(8,128)(2,1)S(1)} collective-permute-done((bf16[2,72,1280]{2,1,0:T(8,128)(2,1)S(1)}, bf16[2,72,1280]{2,1,0:T(8,128)(2,1)S(1)}, u32[]{:S(2)}, u32[]{:S(2)}) %collective-permute-start.29) | collective-permute-done | bytes 368672 | tf_op jit(solution)/shard_map/ppermute | solution.py:32
  146.3 1.8 %add_terms.1 = bf16[128,2560]{1,0:T(8,128)(2,1)} custom-call(f32[8,128]{1,0:T(8,128)S(1)} %get-tuple-element.87.weight_ref, f32[8,128]{1,0:T(8,128)S(1)} %get-tuple-element.88.rank_ref, bf16[128,2560]{1,0:T(8,128)(2,1)S(1)} %bitcast.60, bf16[2,72,1280]{2,1,0:T(8,128)(2,1)S(1)} %get-tuple-element.120.refs_0_, ...), custom_call_target="tpu_custom_call" | custom-call | flops 188743680 | bytes 3276800 | tf_op jit(solution)/shard_map/add_terms/pallas_call | solution.py:289
  (88 shorter events, 5.9 us)
Async XLA Ops:
  0.0 9.8 %copy-start = (bf16[8,128,512]{2,1,0:T(8,128)(2,1)S(1)}, bf16[8,128,512]{2,1,0:T(8,128)(2,1)}, u32[]{:S(2)}) copy-start(bf16[8,128,512]{2,1,0:T(8,128)(2,1)} %param.11) | copy-start | bytes 3145732
  0.0 1.2 copy-start.1
  2.8 14.2 %copy-start.17 = (bf16[2,72,1280]{2,1,0:T(8,128)(2,1)}, bf16[2,72,1280]{2,1,0:T(8,128)(2,1)S(1)}, u32[]{:S(2)}) copy-start(bf16[2,72,1280]{2,1,0:T(8,128)(2,1)S(1)} %get-tuple-element.83) | copy-start | bytes 1105924
  2.9 10.4 %collective-permute-start.2 = (bf16[2,72,1280]{2,1,0:T(8,128)(2,1)S(1)}, bf16[2,72,1280]{2,1,0:T(8,128)(2,1)S(1)}, u32[]{:S(2)}, u32[]{:S(2)}) collective-permute-start(bf16[2,72,1280]{2,1,0:T(8,128)(2,1)S(1)} %get-tuple-element.89.own_ref), channel_id=1, source_target_pairs={{0,1},{1,2},{2,3},{3,0},{4,5},{5,6},{6,7},{7,4},{8,9},{9,10},{10,1... | collective-permute-start | bytes 1105928 | tf_op jit(solution)/shard_map/ppermute | solution.py:32
  5.1 9.4 %collective-permute-start.3 = (bf16[2,72,1280]{2,1,0:T(8,128)(2,1)S(1)}, bf16[2,72,1280]{2,1,0:T(8,128)(2,1)S(1)}, u32[]{:S(2)}, u32[]{:S(2)}) collective-permute-start(bf16[2,72,1280]{2,1,0:T(8,128)(2,1)S(1)} %get-tuple-element.89.own_ref), channel_id=1, source_target_pairs={{0,3},{1,0},{2,1},{3,2},{4,7},{5,4},{6,5},{7,6},{8,11},{9,8},{10,9... | collective-permute-start | bytes 1105928 | tf_op jit(solution)/shard_map/ppermute | solution.py:32
  5.1 10.8 %collective-permute-start = (bf16[2,72,1280]{2,1,0:T(8,128)(2,1)S(1)}, bf16[2,72,1280]{2,1,0:T(8,128)(2,1)S(1)}, u32[]{:S(2)}, u32[]{:S(2)}) collective-permute-start(bf16[2,72,1280]{2,1,0:T(8,128)(2,1)S(1)} %get-tuple-element.72), channel_id=1, source_target_pairs={{0,4},{1,5},{2,6},{3,7},{4,8},{5,9},{6,10},{7,11},{8,12},{9,13},{1... | collective-permute-start | bytes 1105928 | tf_op jit(solution)/shard_map/ppermute | solution.py:32
  6.5 9.5 %collective-permute-start.1 = (bf16[2,72,1280]{2,1,0:T(8,128)(2,1)S(1)}, bf16[2,72,1280]{2,1,0:T(8,128)(2,1)S(1)}, u32[]{:S(2)}, u32[]{:S(2)}) collective-permute-start(bf16[2,72,1280]{2,1,0:T(8,128)(2,1)S(1)} %get-tuple-element.73), channel_id=1, source_target_pairs={{0,12},{1,13},{2,14},{3,15},{4,0},{5,1},{6,2},{7,3},{8,4},{9,5},{1... | collective-permute-start | bytes 1105928 | tf_op jit(solution)/shard_map/ppermute | solution.py:32
  13.3 0.7 copy-start.13
  14.6 0.8 copy-start.15
  16.0 21.9 %collective-permute-start.6 = (bf16[864,1280]{1,0:T(8,128)(2,1)}, bf16[864,1280]{1,0:T(8,128)(2,1)}, u32[]{:S(2)}, u32[]{:S(2)}) collective-permute-start(bf16[864,1280]{1,0:T(8,128)(2,1)} %bitcast.65), channel_id=1, source_target_pairs={{0,128},{128,0},{1,129},{129,1},{2,130},{130,2},{3,131},{131,3},{4... | collective-permute-start | bytes 6635528 | tf_op jit(solution)/shard_map/ppermute | solution.py:362
  16.0 21.9 %collective-permute-start.7 = (bf16[864,1280]{1,0:T(8,128)(2,1)}, bf16[864,1280]{1,0:T(8,128)(2,1)}, u32[]{:S(2)}, u32[]{:S(2)}) collective-permute-start(bf16[864,1280]{1,0:T(8,128)(2,1)} %bitcast.69), channel_id=1, source_target_pairs={{0,128},{128,0},{1,129},{129,1},{2,130},{130,2},{3,131},{131,3},{4... | collective-permute-start | bytes 6635528 | tf_op jit(solution)/shard_map/ppermute | solution.py:362
  16.5 21.4 %collective-permute-start.8 = (bf16[864,1280]{1,0:T(8,128)(2,1)}, bf16[864,1280]{1,0:T(8,128)(2,1)}, u32[]{:S(2)}, u32[]{:S(2)}) collective-permute-start(bf16[864,1280]{1,0:T(8,128)(2,1)} %refs_5_.1), channel_id=1, source_target_pairs={{0,128},{128,0},{1,129},{129,1},{2,130},{130,2},{3,131},{131,3},{4... | collective-permute-start | bytes 6635528 | tf_op jit(solution)/shard_map/ppermute | solution.py:362
  17.1 18.2 %collective-permute-start.4 = (bf16[2,136,1280]{2,1,0:T(8,128)(2,1)S(1)}, bf16[2,136,1280]{2,1,0:T(8,128)(2,1)S(1)}, u32[]{:S(2)}, u32[]{:S(2)}) collective-permute-start(bf16[2,136,1280]{2,1,0:T(8,128)(2,1)S(1)} %pack.1.own_ref), channel_id=1, source_target_pairs={{0,1},{1,2},{2,3},{3,0},{4,5},{5,6},{6,7},{7,4},{8,9},{9,10},{10,1... | collective-permute-start | bytes 2088968 | tf_op jit(solution)/shard_map/ppermute | solution.py:32
  18.8 19.1 %collective-permute-start.5 = (bf16[2,136,1280]{2,1,0:T(8,128)(2,1)S(1)}, bf16[2,136,1280]{2,1,0:T(8,128)(2,1)}, u32[]{:S(2)}, u32[]{:S(2)}) collective-permute-start(bf16[2,136,1280]{2,1,0:T(8,128)(2,1)S(1)} %pack.1.own_ref), channel_id=1, source_target_pairs={{0,3},{1,0},{2,1},{3,2},{4,7},{5,4},{6,5},{7,6},{8,11},{9,8},{10,9... | collective-permute-start | bytes 2088968 | tf_op jit(solution)/shard_map/ppermute | solution.py:32
  38.7 18.4 %collective-permute-start.10 = (bf16[136,1280]{1,0:T(8,128)(2,1)}, bf16[136,1280]{1,0:T(8,128)(2,1)}, u32[]{:S(2)}, u32[]{:S(2)}) collective-permute-start(bf16[136,1280]{1,0:T(8,128)(2,1)} %slice_bitcast_fusion.3), channel_id=1, source_target_pairs={{0,1},{1,2},{2,3},{3,0},{4,5},{5,6},{6,7},{7,4},{8,9},{9,10},{10,1... | collective-permute-start | bytes 1044488 | tf_op jit(solution)/shard_map/ppermute | solution.py:32
  38.9 18.2 %collective-permute-start.9 = (bf16[2,72,1280]{2,1,0:T(8,128)(2,1)}, bf16[2,72,1280]{2,1,0:T(8,128)(2,1)}, u32[]{:S(2)}, u32[]{:S(2)}) collective-permute-start(bf16[2,72,1280]{2,1,0:T(8,128)(2,1)} %copy-done.17), channel_id=1, source_target_pairs={{0,8},{1,9},{2,10},{3,11},{4,12},{5,13},{6,14},{7,15},{8,0},{9,1},... | collective-permute-start | bytes 1105928 | tf_op jit(solution)/shard_map/ppermute | solution.py:32
  43.6 13.5 %collective-permute-start.11 = (bf16[136,1280]{1,0:T(8,128)(2,1)}, bf16[136,1280]{1,0:T(8,128)(2,1)}, u32[]{:S(2)}, u32[]{:S(2)}) collective-permute-start(bf16[136,1280]{1,0:T(8,128)(2,1)} %slice_bitcast_fusion.2), channel_id=1, source_target_pairs={{0,3},{1,0},{2,1},{3,2},{4,7},{5,4},{6,5},{7,6},{8,11},{9,8},{10,9... | collective-permute-start | bytes 1044488 | tf_op jit(solution)/shard_map/ppermute | solution.py:32
  46.0 11.0 %all-to-all-start.1 = ((f32[16,1,320]{2,1,0:T(1,128)}), f32[16,1,320]{2,1,0:T(1,128)S(1)}, u32[]{:S(2)}, u32[]{:S(2)}) async-start(f32[16,1,320]{2,1,0:T(1,128)} %broadcast_in_dim.7), calls=%async_computation.1 | async-start | bytes 49152 | tf_op jit(solution)/shard_map/all_to_all | solution.py:324
  57.1 25.3 %collective-permute-start.13 = (bf16[2,72,1280]{2,1,0:T(8,128)(2,1)}, bf16[2,72,1280]{2,1,0:T(8,128)(2,1)S(1)}, u32[]{:S(2)}, u32[]{:S(2)}) collective-permute-start(bf16[2,72,1280]{2,1,0:T(8,128)(2,1)} %collective-permute-done.9.own_ref), channel_id=1, source_target_pairs={{0,2},{1,3},{2,0},{3,1},{4,6},{5,7},{6,4},{7,5},{8,10},{9,11},{10,... | collective-permute-start | bytes 1105928 | tf_op jit(solution)/shard_map/ppermute | solution.py:32
  59.1 23.3 %collective-permute-start.14 = (bf16[2,72,1280]{2,1,0:T(8,128)(2,1)}, bf16[2,72,1280]{2,1,0:T(8,128)(2,1)S(1)}, u32[]{:S(2)}, u32[]{:S(2)}) collective-permute-start(bf16[2,72,1280]{2,1,0:T(8,128)(2,1)} %collective-permute-done.9.own_ref), channel_id=1, source_target_pairs={{0,1},{1,2},{2,3},{3,0},{4,5},{5,6},{6,7},{7,4},{8,9},{9,10},{10,1... | collective-permute-start | bytes 1105928 | tf_op jit(solution)/shard_map/ppermute | solution.py:32
  60.5 22.0 %collective-permute-start.15 = (bf16[2,72,1280]{2,1,0:T(8,128)(2,1)}, bf16[2,72,1280]{2,1,0:T(8,128)(2,1)S(1)}, u32[]{:S(2)}, u32[]{:S(2)}) collective-permute-start(bf16[2,72,1280]{2,1,0:T(8,128)(2,1)} %collective-permute-done.9.own_ref), channel_id=1, source_target_pairs={{0,3},{1,0},{2,1},{3,2},{4,7},{5,4},{6,5},{7,6},{8,11},{9,8},{10,9... | collective-permute-start | bytes 1105928 | tf_op jit(solution)/shard_map/ppermute | solution.py:32
  61.1 21.3 %collective-permute-start.12 = (bf16[2,72,1280]{2,1,0:T(8,128)(2,1)S(1)}, bf16[2,72,1280]{2,1,0:T(8,128)(2,1)S(1)}, u32[]{:S(2)}, u32[]{:S(2)}) collective-permute-start(bf16[2,72,1280]{2,1,0:T(8,128)(2,1)S(1)} %get-tuple-element.89.own_ref), channel_id=1, source_target_pairs={{0,2},{1,3},{2,0},{3,1},{4,6},{5,7},{6,4},{7,5},{8,10},{9,11},{10,... | collective-permute-start | bytes 1105928 | tf_op jit(solution)/shard_map/ppermute | solution.py:32
  62.8 1.6 %copy-start.7 = (bf16[1280,864]{0,1:T(8,128)(2,1)S(1)}, bf16[1280,864]{0,1:T(8,128)(2,1)}, u32[]{:S(2)}) copy-start(bf16[1280,864]{0,1:T(8,128)(2,1)} %param.15) | copy-start | bytes 6635524
  64.4 1.6 %copy-start.9 = (bf16[1280,864]{0,1:T(8,128)(2,1)S(1)}, bf16[1280,864]{0,1:T(8,128)(2,1)}, u32[]{:S(2)}) copy-start(bf16[1280,864]{0,1:T(8,128)(2,1)} %param.16) | copy-start | bytes 6635524
  66.0 1.6 %copy-start.11 = (bf16[864,1280]{1,0:T(8,128)(2,1)S(1)}, bf16[864,1280]{1,0:T(8,128)(2,1)}, u32[]{:S(2)}) copy-start(bf16[864,1280]{1,0:T(8,128)(2,1)} %refs_5_.1) | copy-start | bytes 6635524
  82.5 12.9 %collective-permute-start.16 = (bf16[136,1280]{1,0:T(8,128)(2,1)S(1)}, bf16[136,1280]{1,0:T(8,128)(2,1)S(1)}, u32[]{:S(2)}, u32[]{:S(2)}) collective-permute-start(bf16[136,1280]{1,0:T(8,128)(2,1)S(1)} %get-tuple-element.140), channel_id=1, source_target_pairs={{0,3},{1,0},{2,1},{3,2},{4,7},{5,4},{6,5},{7,6},{8,11},{9,8},{10,9... | collective-permute-start | bytes 1044488 | tf_op jit(solution)/shard_map/ppermute | solution.py:32
  83.6 11.8 %collective-permute-start.17 = (bf16[136,1280]{1,0:T(8,128)(2,1)S(1)}, bf16[136,1280]{1,0:T(8,128)(2,1)S(1)}, u32[]{:S(2)}, u32[]{:S(2)}) collective-permute-start(bf16[136,1280]{1,0:T(8,128)(2,1)S(1)} %get-tuple-element.139), channel_id=1, source_target_pairs={{0,1},{1,2},{2,3},{3,0},{4,5},{5,6},{6,7},{7,4},{8,9},{9,10},{10,1... | collective-permute-start | bytes 1044488 | tf_op jit(solution)/shard_map/ppermute | solution.py:32
  85.8 15.5 %copy-start.16 = (bf16[2,72,1280]{2,1,0:T(8,128)(2,1)S(1)}, bf16[2,72,1280]{2,1,0:T(8,128)(2,1)}, u32[]{:S(2)}) copy-start(bf16[2,72,1280]{2,1,0:T(8,128)(2,1)} %copy-done.15) | copy-start | bytes 1105924
  95.4 5.9 %copy-start.12 = (bf16[864,1280]{1,0:T(8,128)(2,1)S(1)}, bf16[864,1280]{1,0:T(8,128)(2,1)}, u32[]{:S(2)}) copy-start(bf16[864,1280]{1,0:T(8,128)(2,1)} %refs_5_.1) | copy-start | bytes 6635524
  95.5 5.8 %copy-start.14 = (bf16[2,72,1280]{2,1,0:T(8,128)(2,1)S(1)}, bf16[2,72,1280]{2,1,0:T(8,128)(2,1)}, u32[]{:S(2)}) copy-start(bf16[2,72,1280]{2,1,0:T(8,128)(2,1)} %copy-done.13) | copy-start | bytes 1105924
  95.6 5.8 %copy-start.8 = (bf16[1280,864]{0,1:T(8,128)(2,1)S(1)}, bf16[1280,864]{0,1:T(8,128)(2,1)}, u32[]{:S(2)}) copy-start(bf16[1280,864]{0,1:T(8,128)(2,1)} %param.15) | copy-start | bytes 6635524
  95.6 5.8 %copy-start.10 = (bf16[1280,864]{0,1:T(8,128)(2,1)S(1)}, bf16[1280,864]{0,1:T(8,128)(2,1)}, u32[]{:S(2)}) copy-start(bf16[1280,864]{0,1:T(8,128)(2,1)} %param.16) | copy-start | bytes 6635524
  95.6 20.7 %collective-permute-start.19 = (bf16[2,136,1280]{2,1,0:T(8,128)(2,1)S(1)}, bf16[2,136,1280]{2,1,0:T(8,128)(2,1)S(1)}, u32[]{:S(2)}, u32[]{:S(2)}) collective-permute-start(bf16[2,136,1280]{2,1,0:T(8,128)(2,1)S(1)} %pad_maximum_fusion.1), channel_id=1, source_target_pairs={{0,1},{1,2},{2,3},{3,0},{4,5},{5,6},{6,7},{7,4},{8,9},{9,10},{10,1... | collective-permute-start | bytes 2088968 | tf_op jit(solution)/shard_map/ppermute | solution.py:32
  96.7 19.6 %collective-permute-start.18 = (bf16[2,136,1280]{2,1,0:T(8,128)(2,1)S(1)}, bf16[2,136,1280]{2,1,0:T(8,128)(2,1)S(1)}, u32[]{:S(2)}, u32[]{:S(2)}) collective-permute-start(bf16[2,136,1280]{2,1,0:T(8,128)(2,1)S(1)} %pad_maximum_fusion), channel_id=1, source_target_pairs={{0,3},{1,0},{2,1},{3,2},{4,7},{5,4},{6,5},{7,6},{8,11},{9,8},{10,9... | collective-permute-start | bytes 2088968 | tf_op jit(solution)/shard_map/ppermute | solution.py:32
  98.0 18.3 %collective-permute-start.20 = (bf16[72,1280]{1,0:T(8,128)(2,1)S(1)}, bf16[72,1280]{1,0:T(8,128)(2,1)S(1)}, u32[]{:S(2)}, u32[]{:S(2)}) collective-permute-start(bf16[72,1280]{1,0:T(8,128)(2,1)S(1)} %get-tuple-element.142), channel_id=1, source_target_pairs={{0,3},{1,0},{2,1},{3,2},{4,7},{5,4},{6,5},{7,6},{8,11},{9,8},{10,9... | collective-permute-start | bytes 552968 | tf_op jit(solution)/shard_map/ppermute | solution.py:32
  98.1 18.2 %collective-permute-start.21 = (bf16[72,1280]{1,0:T(8,128)(2,1)S(1)}, bf16[72,1280]{1,0:T(8,128)(2,1)S(1)}, u32[]{:S(2)}, u32[]{:S(2)}) collective-permute-start(bf16[72,1280]{1,0:T(8,128)(2,1)S(1)} %get-tuple-element.141), channel_id=1, source_target_pairs={{0,1},{1,2},{2,3},{3,0},{4,5},{5,6},{6,7},{7,4},{8,9},{9,10},{10,1... | collective-permute-start | bytes 552968 | tf_op jit(solution)/shard_map/ppermute | solution.py:32
  116.4 14.1 %collective-permute-start.23 = (bf16[2,72,1280]{2,1,0:T(8,128)(2,1)S(1)}, bf16[2,72,1280]{2,1,0:T(8,128)(2,1)S(1)}, u32[]{:S(2)}, u32[]{:S(2)}) collective-permute-start(bf16[2,72,1280]{2,1,0:T(8,128)(2,1)S(1)} %pad_maximum_fusion.2), channel_id=1, source_target_pairs={{0,3},{1,0},{2,1},{3,2},{4,7},{5,4},{6,5},{7,6},{8,11},{9,8},{10,9... | collective-permute-start | bytes 1105928 | tf_op jit(solution)/shard_map/ppermute | solution.py:32
  117.5 19.8 %copy-start.3 = (bf16[2560,4]{0,1:T(4,128)(2,1)S(1)}, bf16[2560,4]{0,1:T(4,128)(2,1)}, u32[]{:S(2)}) copy-start(bf16[2560,4]{0,1:T(4,128)(2,1)} %param.14) | copy-start | bytes 61444
  117.5 19.8 %copy-start.5 = (s32[1,128,2]{1,2,0:T(2,128)S(1)}, s32[1,128,2]{1,2,0:T(2,128)}, u32[]{:S(2)}) copy-start(s32[1,128,2]{1,2,0:T(2,128)} %param.18) | copy-start | bytes 3076
  117.5 19.8 %copy-start.6 = (s32[1,128,2]{1,2,0:T(2,128)S(1)}, s32[1,128,2]{1,2,0:T(2,128)}, u32[]{:S(2)}) copy-start(s32[1,128,2]{1,2,0:T(2,128)} %param.19) | copy-start | bytes 3076
  117.5 13.0 %collective-permute-start.24 = (bf16[2,72,1280]{2,1,0:T(8,128)(2,1)S(1)}, bf16[2,72,1280]{2,1,0:T(8,128)(2,1)S(1)}, u32[]{:S(2)}, u32[]{:S(2)}) collective-permute-start(bf16[2,72,1280]{2,1,0:T(8,128)(2,1)S(1)} %pad_maximum_fusion.3), channel_id=1, source_target_pairs={{0,1},{1,2},{2,3},{3,0},{4,5},{5,6},{6,7},{7,4},{8,9},{9,10},{10,1... | collective-permute-start | bytes 1105928 | tf_op jit(solution)/shard_map/ppermute | solution.py:32
  120.2 26.1 %copy-start.2 = (bf16[1,128,2560]{2,1,0:T(8,128)(2,1)S(1)}, bf16[1,128,2560]{2,1,0:T(8,128)(2,1)}, u32[]{:S(2)}) copy-start(bf16[1,128,2560]{2,1,0:T(8,128)(2,1)} %param.10) | copy-start | bytes 1966084
  120.3 10.4 %collective-permute-start.25 = (bf16[2,68,1280]{2,1,0:T(8,128)(2,1)S(1)}, bf16[2,68,1280]{2,1,0:T(8,128)(2,1)S(1)}, u32[]{:S(2)}, u32[]{:S(2)}) collective-permute-start(bf16[2,68,1280]{2,1,0:T(8,128)(2,1)S(1)} %get-tuple-element.138), channel_id=1, source_target_pairs={{0,12},{1,13},{2,14},{3,15},{4,0},{5,1},{6,2},{7,3},{8,4},{9,5},{1... | collective-permute-start | bytes 1044488 | tf_op jit(solution)/shard_map/ppermute | solution.py:32
  121.4 12.7 %collective-permute-start.26 = (bf16[2,68,1280]{2,1,0:T(8,128)(2,1)S(1)}, bf16[2,68,1280]{2,1,0:T(8,128)(2,1)S(1)}, u32[]{:S(2)}, u32[]{:S(2)}) collective-permute-start(bf16[2,68,1280]{2,1,0:T(8,128)(2,1)S(1)} %get-tuple-element.137), channel_id=1, source_target_pairs={{0,4},{1,5},{2,6},{3,7},{4,8},{5,9},{6,10},{7,11},{8,12},{9,13},{1... | collective-permute-start | bytes 1044488 | tf_op jit(solution)/shard_map/ppermute | solution.py:32
  122.4 15.2 %collective-permute-start.22 = (bf16[2,72,1280]{2,1,0:T(8,128)(2,1)S(1)}, bf16[2,72,1280]{2,1,0:T(8,128)(2,1)S(1)}, u32[]{:S(2)}, u32[]{:S(2)}) collective-permute-start(bf16[2,72,1280]{2,1,0:T(8,128)(2,1)S(1)} %get-tuple-element.121), channel_id=1, source_target_pairs={{0,2},{1,3},{2,0},{3,1},{4,6},{5,7},{6,4},{7,5},{8,10},{9,11},{10,... | collective-permute-start | bytes 1105928 | tf_op jit(solution)/shard_map/ppermute | solution.py:32
  134.0 8.7 %collective-permute-start.27 = (bf16[2,72,1280]{2,1,0:T(8,128)(2,1)S(1)}, bf16[2,72,1280]{2,1,0:T(8,128)(2,1)S(1)}, u32[]{:S(2)}, u32[]{:S(2)}) collective-permute-start(bf16[2,72,1280]{2,1,0:T(8,128)(2,1)S(1)} %get-tuple-element.132), channel_id=1, source_target_pairs={{0,3},{1,0},{2,1},{3,2},{4,7},{5,4},{6,5},{7,6},{8,11},{9,8},{10,9... | collective-permute-start | bytes 1105928 | tf_op jit(solution)/shard_map/ppermute | solution.py:32
  134.3 8.4 %collective-permute-start.28 = (bf16[2,72,1280]{2,1,0:T(8,128)(2,1)S(1)}, bf16[2,72,1280]{2,1,0:T(8,128)(2,1)S(1)}, u32[]{:S(2)}, u32[]{:S(2)}) collective-permute-start(bf16[2,72,1280]{2,1,0:T(8,128)(2,1)S(1)} %get-tuple-element.133), channel_id=1, source_target_pairs={{0,1},{1,2},{2,3},{3,0},{4,5},{5,6},{6,7},{7,4},{8,9},{9,10},{10,1... | collective-permute-start | bytes 1105928 | tf_op jit(solution)/shard_map/ppermute | solution.py:32
  137.3 9.0 %collective-permute-start.29 = (bf16[2,72,1280]{2,1,0:T(8,128)(2,1)S(1)}, bf16[2,72,1280]{2,1,0:T(8,128)(2,1)S(1)}, u32[]{:S(2)}, u32[]{:S(2)}) collective-permute-start(bf16[2,72,1280]{2,1,0:T(8,128)(2,1)S(1)} %add_convert_fusion.1), channel_id=1, source_target_pairs={{0,8},{1,9},{2,10},{3,11},{4,12},{5,13},{6,14},{7,15},{8,0},{9,1},... | collective-permute-start | bytes 1105928 | tf_op jit(solution)/shard_map/ppermute | solution.py:32
  (1 other events, 0.7 us)

commit v2 on v1

--- a/solution.py
+++ b/solution.py
@@ -361,14 +361,16 @@
     owns = tie((gate_weight.T, up_weight.T, down_weight, from_up))[:3]
     swapped = [lax.ppermute(own, "dp", swap) for own in owns]
     columns = jnp.sum(exchange(partial_value, "seq"), axis=0, keepdims=True)
+    columns = jnp.broadcast_to(columns, (owners, columns.shape[1]))
     columns, outer, *rest = tie((columns, bins[2], *near, *swapped))
     near, swapped = rest[:2], rest[2:]
     weights = [owns[0], swapped[0], owns[1], swapped[1], owns[2], swapped[2]]
 
     far = shift(near[0][0], right_of), shift(near[1][1], left_of)
     outer = shift(outer, along_y(2))
-    modulation = exchange(jnp.broadcast_to(columns, (owners, columns.shape[1]))).reshape(2, width)
+    modulation = exchange(columns)
     modulation, outer, middle, *far = tie((modulation, outer, middle, *far))
+    modulation = modulation.reshape(2, width)
 
     outer_near, outer_far = both_ways(outer), shift(outer, across_x)
     middle_far = shift(middle, across_x)

time: 149 us -> 149 us (level)
    unnamed x36 -> x37, local copies, waits for them, and re-layouts: 8.3 us -> 8.31 us
where the time goes in v2:
time: 149 us; the launch traced here: 148 us
  starting transfers between devices  41.7 us (28%)
  waiting for transfers between devices  38.1 us (26%)
  Pallas kernels  36.9 us (25%)
  blocking collectives  16 us (11%)
  local copies, waits for them, and re-layouts  11.8 us (8%)
  other arithmetic  2.19 us (1%)
    ppermute x27, starting transfers between devices, shift(): return lax.ppermute(value, 'expert', perm)  35.9 us
    pallas_call x3, Pallas kernels, run_expert(): pl.pallas_call(expert_kernel, out_shape=[jax.ShapeDtypeStruct(own.shape,...  33.2 us
    ppermute x27, waiting for transfers between devices, shift(): return lax.ppermute(value, 'expert', perm)  32.4 us
    all_to_all x1, blocking collectives, exchange(): return lax.all_to_all(value, axis, split_axis=0, concat_axis=0, tiled=True)  16 us
    unnamed x37, local copies, waits for them, and re-layouts  8.31 us
    all_to_all x1, waiting for transfers between devices, exchange(): return lax.all_to_all(value, axis, split_axis=0, concat_axis=0, tiled=True)  5.63 us
    all_to_all x1, starting transfers between devices, exchange(): return lax.all_to_all(value, axis, split_axis=0, concat_axis=0, tiled=True)  5.31 us
  transfers between devices with their start and end apart: 31, of which 11 were waited for; matrix products, arithmetic and copies ran while one was open for 4% of the time, Pallas kernels for 23%

profile of v2, /device:TPU:6, one launch (start us, length us, event | category | flops | bytes accessed | tf_op | source)
XLA Modules:
  0.0 148.4 jit_solution(15927569187541495610)
XLA Ops:
  0.0 1.2 copy-done.1
  1.2 0.7 copy-done.4
  1.9 1.0 normalise_and_bin.1
  2.9 2.3 %collective-permute-start.2 = (bf16[2,72,1280]{2,1,0:T(8,128)(2,1)S(1)}, bf16[2,72,1280]{2,1,0:T(8,128)(2,1)S(1)}, u32[]{:S(2)}, u32[]{:S(2)}) collective-permute-start(bf16[2,72,1280]{2,1,0:T(8,128)(2,1)S(1)} %get-tuple-element.89.own_ref), channel_id=1, source_target_pairs={{0,1},{1,2},{2,3},{3,0},{4,5},{5,6},{6,7},{7,4},{8,9},{9,10},{10,1... | collective-permute-start | bytes 1105928 | tf_op jit(solution)/shard_map/ppermute | solution.py:32
  5.1 1.4 collective-permute-start
  6.5 1.8 %collective-permute-start.1 = (bf16[2,72,1280]{2,1,0:T(8,128)(2,1)S(1)}, bf16[2,72,1280]{2,1,0:T(8,128)(2,1)S(1)}, u32[]{:S(2)}, u32[]{:S(2)}) collective-permute-start(bf16[2,72,1280]{2,1,0:T(8,128)(2,1)S(1)} %get-tuple-element.73), channel_id=1, source_target_pairs={{0,12},{1,13},{2,14},{3,15},{4,0},{5,1},{6,2},{7,3},{8,4},{9,5},{1... | collective-permute-start | bytes 1105928 | tf_op jit(solution)/shard_map/ppermute | solution.py:32
  8.4 0.7 fusion.10
  9.1 0.7 convert_element_type.31
  10.0 1.2 fusion.7
  11.2 2.1 %collective-permute-done.2.left_ref = bf16[2,72,1280]{2,1,0:T(8,128)(2,1)S(1)} collective-permute-done((bf16[2,72,1280]{2,1,0:T(8,128)(2,1)S(1)}, bf16[2,72,1280]{2,1,0:T(8,128)(2,1)S(1)}, u32[]{:S(2)}, u32[]{:S(2)}) %collective-permute-start.2) | collective-permute-done | bytes 368672 | tf_op jit(solution)/shard_map/ppermute | solution.py:32
  13.3 0.7 copy-done.13
  14.6 0.8 copy-done.15
  17.1 1.8 %collective-permute-start.4 = (bf16[2,136,1280]{2,1,0:T(8,128)(2,1)S(1)}, bf16[2,136,1280]{2,1,0:T(8,128)(2,1)S(1)}, u32[]{:S(2)}, u32[]{:S(2)}) collective-permute-start(bf16[2,136,1280]{2,1,0:T(8,128)(2,1)S(1)} %pack.1.own_ref), channel_id=1, source_target_pairs={{0,1},{1,2},{2,3},{3,0},{4,5},{5,6},{6,7},{7,4},{8,9},{9,10},{10,1... | collective-permute-start | bytes 2088968 | tf_op jit(solution)/shard_map/ppermute | solution.py:32
  19.2 16.0 %all_to_all.21 = f32[8,1,320]{2,1,0:T(1,128)S(1)} all-to-all(f32[8,1,320]{2,1,0:T(1,128)S(1)} %copy.11), channel_id=1, replica_groups=mesh['dp'=2,'seq'=8,'expert'=16] {'seq'}, dimensions={0} | all-to-all | bytes 20480 | tf_op jit(solution)/shard_map/all_to_all | solution.py:324
  35.2 2.7 %collective-permute-done.5.right_ref = bf16[2,136,1280]{2,1,0:T(8,128)(2,1)} collective-permute-done((bf16[2,136,1280]{2,1,0:T(8,128)(2,1)S(1)}, bf16[2,136,1280]{2,1,0:T(8,128)(2,1)}, u32[]{:S(2)}, u32[]{:S(2)}) %collective-permute-start.5) | collective-permute-done | bytes 696352 | tf_op jit(solution)/shard_map/ppermute | solution.py:32
  37.9 0.8 slice_bitcast_fusion.3
  39.0 2.9 %collective-permute-start.9 = (bf16[2,72,1280]{2,1,0:T(8,128)(2,1)}, bf16[2,72,1280]{2,1,0:T(8,128)(2,1)}, u32[]{:S(2)}, u32[]{:S(2)}) collective-permute-start(bf16[2,72,1280]{2,1,0:T(8,128)(2,1)} %copy-done.17), channel_id=1, source_target_pairs={{0,8},{1,9},{2,10},{3,11},{4,12},{5,13},{6,14},{7,15},{8,0},{9,1},... | collective-permute-start | bytes 1105928 | tf_op jit(solution)/shard_map/ppermute | solution.py:32
  41.9 1.7 %slice_bitcast_fusion.2 = bf16[136,1280]{1,0:T(8,128)(2,1)} fusion(bf16[2,136,1280]{2,1,0:T(8,128)(2,1)} %collective-permute-done.5.right_ref), kind=kLoop, calls=%fused_computation.12 | loop fusion | bytes 696320 | tf_op jit(solution)/shard_map/squeeze | solution.py:369
  43.6 1.8 %collective-permute-start.11 = (bf16[136,1280]{1,0:T(8,128)(2,1)}, bf16[136,1280]{1,0:T(8,128)(2,1)}, u32[]{:S(2)}, u32[]{:S(2)}) collective-permute-start(bf16[136,1280]{1,0:T(8,128)(2,1)} %slice_bitcast_fusion.2), channel_id=1, source_target_pairs={{0,3},{1,0},{2,1},{3,2},{4,7},{5,4},{6,5},{7,6},{8,11},{9,8},{10,9... | collective-permute-start | bytes 1044488 | tf_op jit(solution)/shard_map/ppermute | solution.py:32
  46.0 5.3 %all-to-all-start.1 = ((f32[16,1,320]{2,1,0:T(1,128)}), f32[16,1,320]{2,1,0:T(1,128)S(1)}, u32[]{:S(2)}, u32[]{:S(2)}) async-start(f32[16,1,320]{2,1,0:T(1,128)} %all_to_all.16), calls=%async_computation.1 | async-start | bytes 49152 | tf_op jit(solution)/shard_map/all_to_all | solution.py:324
  51.3 5.6 %all-to-all-done.1 = f32[16,1,320]{2,1,0:T(1,128)S(1)} async-done(((f32[16,1,320]{2,1,0:T(1,128)}), f32[16,1,320]{2,1,0:T(1,128)S(1)}, u32[]{:S(2)}, u32[]{:S(2)}) %all-to-all-start.1) | async-done | bytes 20512 | tf_op jit(solution)/shard_map/all_to_all | solution.py:324
  56.9 2.2 %collective-permute-start.13 = (bf16[2,72,1280]{2,1,0:T(8,128)(2,1)}, bf16[2,72,1280]{2,1,0:T(8,128)(2,1)}, u32[]{:S(2)}, u32[]{:S(2)}) collective-permute-start(bf16[2,72,1280]{2,1,0:T(8,128)(2,1)} %collective-permute-done.9.own_ref), channel_id=1, source_target_pairs={{0,2},{1,3},{2,0},{3,1},{4,6},{5,7},{6,4},{7,5},{8,10},{9,11},{10,... | collective-permute-start | bytes 1105928 | tf_op jit(solution)/shard_map/ppermute | solution.py:32
  59.1 1.2 collective-permute-start.14
  60.3 0.8 collective-permute-start.15
  61.2 1.5 %collective-permute-start.12 = (bf16[2,72,1280]{2,1,0:T(8,128)(2,1)S(1)}, bf16[2,72,1280]{2,1,0:T(8,128)(2,1)S(1)}, u32[]{:S(2)}, u32[]{:S(2)}) collective-permute-start(bf16[2,72,1280]{2,1,0:T(8,128)(2,1)S(1)} %get-tuple-element.89.own_ref), channel_id=1, source_target_pairs={{0,2},{1,3},{2,0},{3,1},{4,6},{5,7},{6,4},{7,5},{8,10},{9,11},{10,... | collective-permute-start | bytes 1105928 | tf_op jit(solution)/shard_map/ppermute | solution.py:32
  62.7 1.6 %copy-done.7 = bf16[1280,864]{0,1:T(8,128)(2,1)S(1)} copy-done((bf16[1280,864]{0,1:T(8,128)(2,1)S(1)}, bf16[1280,864]{0,1:T(8,128)(2,1)}, u32[]{:S(2)}) %copy-start.7) | copy-done | bytes 2211864
  64.4 1.6 %copy-done.9 = bf16[1280,864]{0,1:T(8,128)(2,1)S(1)} copy-done((bf16[1280,864]{0,1:T(8,128)(2,1)S(1)}, bf16[1280,864]{0,1:T(8,128)(2,1)}, u32[]{:S(2)}) %copy-start.9) | copy-done | bytes 2211864
  66.0 1.6 %copy-done.11 = bf16[864,1280]{1,0:T(8,128)(2,1)S(1)} copy-done((bf16[864,1280]{1,0:T(8,128)(2,1)S(1)}, bf16[864,1280]{1,0:T(8,128)(2,1)}, u32[]{:S(2)}) %copy-start.11) | copy-done | bytes 2211864
  67.6 14.0 %expert_units.3 = (bf16[2,136,1280]{2,1,0:T(8,128)(2,1)S(1)}, bf16[2,136,1280]{2,1,0:T(8,128)(2,1)S(1)}, bf16[2,136,1280]{2,1,0:T(8,128)(2,1)S(1)}, bf16[2,136,1280]{2,1,0:T(8,128)(2,1)S(1)}) custom-call(s32[1]{0:T(128)} %bitcast.15.dp_ref, f32[2,2560]{1,0:T(2,128)S(1)} %reshape.17.mod_ref, bf16[2,136,1280]{2,1,0:T(8,128)(2,1)S(1)} %pack.1.own_ref, ...), custom_call_target="tpu_custom_call" | custom-call | flops 14438891520 | bytes 18841600 | tf_op jit(solution)/shard_map/expert_units/pallas_call | solution.py:197
  81.6 0.7 collective-permute-done.12.refs_0_
  82.4 1.3 collective-permute-start.16
  83.6 2.0 %collective-permute-start.17 = (bf16[136,1280]{1,0:T(8,128)(2,1)S(1)}, bf16[136,1280]{1,0:T(8,128)(2,1)S(1)}, u32[]{:S(2)}, u32[]{:S(2)}) collective-permute-start(bf16[136,1280]{1,0:T(8,128)(2,1)S(1)} %get-tuple-element.139), channel_id=1, source_target_pairs={{0,1},{1,2},{2,3},{3,0},{4,5},{5,6},{6,7},{7,4},{8,9},{9,10},{10,1... | collective-permute-start | bytes 1044488 | tf_op jit(solution)/shard_map/ppermute | solution.py:32
  85.7 9.9 %expert_units.4 = (bf16[2,72,1280]{2,1,0:T(8,128)(2,1)S(1)}, bf16[2,72,1280]{2,1,0:T(8,128)(2,1)S(1)}, bf16[2,72,1280]{2,1,0:T(8,128)(2,1)S(1)}, bf16[2,72,1280]{2,1,0:T(8,128)(2,1)S(1)}) custom-call(s32[1]{0:T(128)} %bitcast.15.dp_ref, f32[2,2560]{1,0:T(2,128)S(1)} %reshape.17.mod_ref, bf16[2,72,1280]{2,1,0:T(8,128)(2,1)} %collective-permute-done.9.own_ref, ...), custom_call_target="tpu_custom_call" | custom-call | flops 7644119040 | bytes 16220160 | tf_op jit(solution)/shard_map/expert_units/pallas_call | solution.py:197
  95.8 0.9 collective-permute-start.19
  96.8 1.3 collective-permute-start.18
  98.2 3.2 %collective-permute-start.21 = (bf16[72,1280]{1,0:T(8,128)(2,1)S(1)}, bf16[72,1280]{1,0:T(8,128)(2,1)S(1)}, u32[]{:S(2)}, u32[]{:S(2)}) collective-permute-start(bf16[72,1280]{1,0:T(8,128)(2,1)S(1)} %get-tuple-element.141), channel_id=1, source_target_pairs={{0,1},{1,2},{2,3},{3,0},{4,5},{5,6},{6,7},{7,4},{8,9},{9,10},{10,1... | collective-permute-start | bytes 552968 | tf_op jit(solution)/shard_map/ppermute | solution.py:32
  101.5 9.4 %expert_units.5 = (bf16[2,72,1280]{2,1,0:T(8,128)(2,1)S(1)}, bf16[2,72,1280]{2,1,0:T(8,128)(2,1)S(1)}, bf16[2,72,1280]{2,1,0:T(8,128)(2,1)S(1)}, bf16[2,72,1280]{2,1,0:T(8,128)(2,1)S(1)}) custom-call(s32[1]{0:T(128)} %bitcast.15.dp_ref, f32[2,2560]{1,0:T(2,128)S(1)} %reshape.17.mod_ref, bf16[2,72,1280]{2,1,0:T(8,128)(2,1)S(1)} %get-tuple-element.89.own_ref, ...), custom_call_target="tpu_custom_call" | custom-call | flops 7644119040 | bytes 16220160 | tf_op jit(solution)/shard_map/expert_units/pallas_call | solution.py:197
  110.9 5.5 %collective-permute-done.20 = bf16[72,1280]{1,0:T(8,128)(2,1)S(1)} collective-permute-done((bf16[72,1280]{1,0:T(8,128)(2,1)S(1)}, bf16[72,1280]{1,0:T(8,128)(2,1)S(1)}, u32[]{:S(2)}, u32[]{:S(2)}) %collective-permute-start.20) | collective-permute-done | bytes 184352 | tf_op jit(solution)/shard_map/ppermute | solution.py:32
  116.5 1.1 collective-permute-start.23
  117.7 2.3 %collective-permute-start.24 = (bf16[2,72,1280]{2,1,0:T(8,128)(2,1)S(1)}, bf16[2,72,1280]{2,1,0:T(8,128)(2,1)S(1)}, u32[]{:S(2)}, u32[]{:S(2)}) collective-permute-start(bf16[2,72,1280]{2,1,0:T(8,128)(2,1)S(1)} %pad_maximum_fusion.3), channel_id=1, source_target_pairs={{0,1},{1,2},{2,3},{3,0},{4,5},{5,6},{6,7},{7,4},{8,9},{9,10},{10,1... | collective-permute-start | bytes 1105928 | tf_op jit(solution)/shard_map/ppermute | solution.py:32
  120.4 1.2 collective-permute-start.25
  121.6 0.9 collective-permute-start.26
  122.6 8.4 %collective-permute-done.23 = bf16[2,72,1280]{2,1,0:T(8,128)(2,1)S(1)} collective-permute-done((bf16[2,72,1280]{2,1,0:T(8,128)(2,1)S(1)}, bf16[2,72,1280]{2,1,0:T(8,128)(2,1)S(1)}, u32[]{:S(2)}, u32[]{:S(2)}) %collective-permute-start.23) | collective-permute-done | bytes 368672 | tf_op jit(solution)/shard_map/ppermute | solution.py:32
  131.1 3.2 %collective-permute-done.26.refs_5_ = bf16[2,68,1280]{2,1,0:T(8,128)(2,1)S(1)} collective-permute-done((bf16[2,68,1280]{2,1,0:T(8,128)(2,1)S(1)}, bf16[2,68,1280]{2,1,0:T(8,128)(2,1)S(1)}, u32[]{:S(2)}, u32[]{:S(2)}) %collective-permute-start.26) | collective-permute-done | bytes 348192 | tf_op jit(solution)/shard_map/ppermute | solution.py:32
  134.3 3.2 %collective-permute-start.28 = (bf16[2,72,1280]{2,1,0:T(8,128)(2,1)S(1)}, bf16[2,72,1280]{2,1,0:T(8,128)(2,1)S(1)}, u32[]{:S(2)}, u32[]{:S(2)}) collective-permute-start(bf16[2,72,1280]{2,1,0:T(8,128)(2,1)S(1)} %get-tuple-element.133), channel_id=1, source_target_pairs={{0,1},{1,2},{2,3},{3,0},{4,5},{5,6},{6,7},{7,4},{8,9},{9,10},{10,1... | collective-permute-start | bytes 1105928 | tf_op jit(solution)/shard_map/ppermute | solution.py:32
  137.9 5.1 %collective-permute-done.27.refs_2_ = bf16[2,72,1280]{2,1,0:T(8,128)(2,1)S(1)} collective-permute-done((bf16[2,72,1280]{2,1,0:T(8,128)(2,1)S(1)}, bf16[2,72,1280]{2,1,0:T(8,128)(2,1)S(1)}, u32[]{:S(2)}, u32[]{:S(2)}) %collective-permute-start.27) | collective-permute-done | bytes 368672 | tf_op jit(solution)/shard_map/ppermute | solution.py:32
  143.0 3.5 %collective-permute-done.29.refs_6_ = bf16[2,72,1280]{2,1,0:T(8,128)(2,1)S(1)} collective-permute-done((bf16[2,72,1280]{2,1,0:T(8,128)(2,1)S(1)}, bf16[2,72,1280]{2,1,0:T(8,128)(2,1)S(1)}, u32[]{:S(2)}, u32[]{:S(2)}) %collective-permute-start.29) | collective-permute-done | bytes 368672 | tf_op jit(solution)/shard_map/ppermute | solution.py:32
  146.6 1.8 %add_terms.1 = bf16[128,2560]{1,0:T(8,128)(2,1)} custom-call(f32[8,128]{1,0:T(8,128)S(1)} %get-tuple-element.87.weight_ref, f32[8,128]{1,0:T(8,128)S(1)} %get-tuple-element.88.rank_ref, bf16[128,2560]{1,0:T(8,128)(2,1)S(1)} %bitcast.63, bf16[2,72,1280]{2,1,0:T(8,128)(2,1)S(1)} %get-tuple-element.120.refs_0_, ...), custom_call_target="tpu_custom_call" | custom-call | flops 188743680 | bytes 3276800 | tf_op jit(solution)/shard_map/add_terms/pallas_call | solution.py:289
  (87 shorter events, 5.5 us)
Async XLA Ops:
  0.0 9.8 %copy-start = (bf16[8,128,512]{2,1,0:T(8,128)(2,1)S(1)}, bf16[8,128,512]{2,1,0:T(8,128)(2,1)}, u32[]{:S(2)}) copy-start(bf16[8,128,512]{2,1,0:T(8,128)(2,1)} %param.11) | copy-start | bytes 3145732
  0.0 1.2 copy-start.1
  2.8 14.2 %copy-start.17 = (bf16[2,72,1280]{2,1,0:T(8,128)(2,1)}, bf16[2,72,1280]{2,1,0:T(8,128)(2,1)S(1)}, u32[]{:S(2)}) copy-start(bf16[2,72,1280]{2,1,0:T(8,128)(2,1)S(1)} %get-tuple-element.83) | copy-start | bytes 1105924
  2.9 10.4 %collective-permute-start.2 = (bf16[2,72,1280]{2,1,0:T(8,128)(2,1)S(1)}, bf16[2,72,1280]{2,1,0:T(8,128)(2,1)S(1)}, u32[]{:S(2)}, u32[]{:S(2)}) collective-permute-start(bf16[2,72,1280]{2,1,0:T(8,128)(2,1)S(1)} %get-tuple-element.89.own_ref), channel_id=1, source_target_pairs={{0,1},{1,2},{2,3},{3,0},{4,5},{5,6},{6,7},{7,4},{8,9},{9,10},{10,1... | collective-permute-start | bytes 1105928 | tf_op jit(solution)/shard_map/ppermute | solution.py:32
  5.1 9.4 %collective-permute-start.3 = (bf16[2,72,1280]{2,1,0:T(8,128)(2,1)S(1)}, bf16[2,72,1280]{2,1,0:T(8,128)(2,1)S(1)}, u32[]{:S(2)}, u32[]{:S(2)}) collective-permute-start(bf16[2,72,1280]{2,1,0:T(8,128)(2,1)S(1)} %get-tuple-element.89.own_ref), channel_id=1, source_target_pairs={{0,3},{1,0},{2,1},{3,2},{4,7},{5,4},{6,5},{7,6},{8,11},{9,8},{10,9... | collective-permute-start | bytes 1105928 | tf_op jit(solution)/shard_map/ppermute | solution.py:32
  5.1 10.8 %collective-permute-start = (bf16[2,72,1280]{2,1,0:T(8,128)(2,1)S(1)}, bf16[2,72,1280]{2,1,0:T(8,128)(2,1)S(1)}, u32[]{:S(2)}, u32[]{:S(2)}) collective-permute-start(bf16[2,72,1280]{2,1,0:T(8,128)(2,1)S(1)} %get-tuple-element.72), channel_id=1, source_target_pairs={{0,4},{1,5},{2,6},{3,7},{4,8},{5,9},{6,10},{7,11},{8,12},{9,13},{1... | collective-permute-start | bytes 1105928 | tf_op jit(solution)/shard_map/ppermute | solution.py:32
  6.5 9.5 %collective-permute-start.1 = (bf16[2,72,1280]{2,1,0:T(8,128)(2,1)S(1)}, bf16[2,72,1280]{2,1,0:T(8,128)(2,1)S(1)}, u32[]{:S(2)}, u32[]{:S(2)}) collective-permute-start(bf16[2,72,1280]{2,1,0:T(8,128)(2,1)S(1)} %get-tuple-element.73), channel_id=1, source_target_pairs={{0,12},{1,13},{2,14},{3,15},{4,0},{5,1},{6,2},{7,3},{8,4},{9,5},{1... | collective-permute-start | bytes 1105928 | tf_op jit(solution)/shard_map/ppermute | solution.py:32
  13.3 0.7 copy-start.13
  14.6 0.8 copy-start.15
  16.0 21.9 %collective-permute-start.6 = (bf16[864,1280]{1,0:T(8,128)(2,1)}, bf16[864,1280]{1,0:T(8,128)(2,1)}, u32[]{:S(2)}, u32[]{:S(2)}) collective-permute-start(bf16[864,1280]{1,0:T(8,128)(2,1)} %bitcast.68), channel_id=1, source_target_pairs={{0,128},{128,0},{1,129},{129,1},{2,130},{130,2},{3,131},{131,3},{4... | collective-permute-start | bytes 6635528 | tf_op jit(solution)/shard_map/ppermute | solution.py:362
  16.0 21.9 %collective-permute-start.7 = (bf16[864,1280]{1,0:T(8,128)(2,1)}, bf16[864,1280]{1,0:T(8,128)(2,1)}, u32[]{:S(2)}, u32[]{:S(2)}) collective-permute-start(bf16[864,1280]{1,0:T(8,128)(2,1)} %bitcast.72), channel_id=1, source_target_pairs={{0,128},{128,0},{1,129},{129,1},{2,130},{130,2},{3,131},{131,3},{4... | collective-permute-start | bytes 6635528 | tf_op jit(solution)/shard_map/ppermute | solution.py:362
  16.5 21.4 %collective-permute-start.8 = (bf16[864,1280]{1,0:T(8,128)(2,1)}, bf16[864,1280]{1,0:T(8,128)(2,1)}, u32[]{:S(2)}, u32[]{:S(2)}) collective-permute-start(bf16[864,1280]{1,0:T(8,128)(2,1)} %refs_5_.1), channel_id=1, source_target_pairs={{0,128},{128,0},{1,129},{129,1},{2,130},{130,2},{3,131},{131,3},{4... | collective-permute-start | bytes 6635528 | tf_op jit(solution)/shard_map/ppermute | solution.py:362
  17.1 18.2 %collective-permute-start.4 = (bf16[2,136,1280]{2,1,0:T(8,128)(2,1)S(1)}, bf16[2,136,1280]{2,1,0:T(8,128)(2,1)S(1)}, u32[]{:S(2)}, u32[]{:S(2)}) collective-permute-start(bf16[2,136,1280]{2,1,0:T(8,128)(2,1)S(1)} %pack.1.own_ref), channel_id=1, source_target_pairs={{0,1},{1,2},{2,3},{3,0},{4,5},{5,6},{6,7},{7,4},{8,9},{9,10},{10,1... | collective-permute-start | bytes 2088968 | tf_op jit(solution)/shard_map/ppermute | solution.py:32
  18.8 19.1 %collective-permute-start.5 = (bf16[2,136,1280]{2,1,0:T(8,128)(2,1)S(1)}, bf16[2,136,1280]{2,1,0:T(8,128)(2,1)}, u32[]{:S(2)}, u32[]{:S(2)}) collective-permute-start(bf16[2,136,1280]{2,1,0:T(8,128)(2,1)S(1)} %pack.1.own_ref), channel_id=1, source_target_pairs={{0,3},{1,0},{2,1},{3,2},{4,7},{5,4},{6,5},{7,6},{8,11},{9,8},{10,9... | collective-permute-start | bytes 2088968 | tf_op jit(solution)/shard_map/ppermute | solution.py:32
  38.7 18.2 %collective-permute-start.10 = (bf16[136,1280]{1,0:T(8,128)(2,1)}, bf16[136,1280]{1,0:T(8,128)(2,1)}, u32[]{:S(2)}, u32[]{:S(2)}) collective-permute-start(bf16[136,1280]{1,0:T(8,128)(2,1)} %slice_bitcast_fusion.3), channel_id=1, source_target_pairs={{0,1},{1,2},{2,3},{3,0},{4,5},{5,6},{6,7},{7,4},{8,9},{9,10},{10,1... | collective-permute-start | bytes 1044488 | tf_op jit(solution)/shard_map/ppermute | solution.py:32
  39.0 18.0 %collective-permute-start.9 = (bf16[2,72,1280]{2,1,0:T(8,128)(2,1)}, bf16[2,72,1280]{2,1,0:T(8,128)(2,1)}, u32[]{:S(2)}, u32[]{:S(2)}) collective-permute-start(bf16[2,72,1280]{2,1,0:T(8,128)(2,1)} %copy-done.17), channel_id=1, source_target_pairs={{0,8},{1,9},{2,10},{3,11},{4,12},{5,13},{6,14},{7,15},{8,0},{9,1},... | collective-permute-start | bytes 1105928 | tf_op jit(solution)/shard_map/ppermute | solution.py:32
  43.6 13.3 %collective-permute-start.11 = (bf16[136,1280]{1,0:T(8,128)(2,1)}, bf16[136,1280]{1,0:T(8,128)(2,1)}, u32[]{:S(2)}, u32[]{:S(2)}) collective-permute-start(bf16[136,1280]{1,0:T(8,128)(2,1)} %slice_bitcast_fusion.2), channel_id=1, source_target_pairs={{0,3},{1,0},{2,1},{3,2},{4,7},{5,4},{6,5},{7,6},{8,11},{9,8},{10,9... | collective-permute-start | bytes 1044488 | tf_op jit(solution)/shard_map/ppermute | solution.py:32
  46.0 10.9 %all-to-all-start.1 = ((f32[16,1,320]{2,1,0:T(1,128)}), f32[16,1,320]{2,1,0:T(1,128)S(1)}, u32[]{:S(2)}, u32[]{:S(2)}) async-start(f32[16,1,320]{2,1,0:T(1,128)} %all_to_all.16), calls=%async_computation.1 | async-start | bytes 49152 | tf_op jit(solution)/shard_map/all_to_all | solution.py:324
  56.9 25.4 %collective-permute-start.13 = (bf16[2,72,1280]{2,1,0:T(8,128)(2,1)}, bf16[2,72,1280]{2,1,0:T(8,128)(2,1)}, u32[]{:S(2)}, u32[]{:S(2)}) collective-permute-start(bf16[2,72,1280]{2,1,0:T(8,128)(2,1)} %collective-permute-done.9.own_ref), channel_id=1, source_target_pairs={{0,2},{1,3},{2,0},{3,1},{4,6},{5,7},{6,4},{7,5},{8,10},{9,11},{10,... | collective-permute-start | bytes 1105928 | tf_op jit(solution)/shard_map/ppermute | solution.py:32
  59.1 23.2 %collective-permute-start.14 = (bf16[2,72,1280]{2,1,0:T(8,128)(2,1)}, bf16[2,72,1280]{2,1,0:T(8,128)(2,1)}, u32[]{:S(2)}, u32[]{:S(2)}) collective-permute-start(bf16[2,72,1280]{2,1,0:T(8,128)(2,1)} %collective-permute-done.9.own_ref), channel_id=1, source_target_pairs={{0,1},{1,2},{2,3},{3,0},{4,5},{5,6},{6,7},{7,4},{8,9},{9,10},{10,1... | collective-permute-start | bytes 1105928 | tf_op jit(solution)/shard_map/ppermute | solution.py:32
  60.3 22.0 %collective-permute-start.15 = (bf16[2,72,1280]{2,1,0:T(8,128)(2,1)}, bf16[2,72,1280]{2,1,0:T(8,128)(2,1)}, u32[]{:S(2)}, u32[]{:S(2)}) collective-permute-start(bf16[2,72,1280]{2,1,0:T(8,128)(2,1)} %collective-permute-done.9.own_ref), channel_id=1, source_target_pairs={{0,3},{1,0},{2,1},{3,2},{4,7},{5,4},{6,5},{7,6},{8,11},{9,8},{10,9... | collective-permute-start | bytes 1105928 | tf_op jit(solution)/shard_map/ppermute | solution.py:32
  61.2 21.1 %collective-permute-start.12 = (bf16[2,72,1280]{2,1,0:T(8,128)(2,1)S(1)}, bf16[2,72,1280]{2,1,0:T(8,128)(2,1)S(1)}, u32[]{:S(2)}, u32[]{:S(2)}) collective-permute-start(bf16[2,72,1280]{2,1,0:T(8,128)(2,1)S(1)} %get-tuple-element.89.own_ref), channel_id=1, source_target_pairs={{0,2},{1,3},{2,0},{3,1},{4,6},{5,7},{6,4},{7,5},{8,10},{9,11},{10,... | collective-permute-start | bytes 1105928 | tf_op jit(solution)/shard_map/ppermute | solution.py:32
  62.7 1.6 %copy-start.7 = (bf16[1280,864]{0,1:T(8,128)(2,1)S(1)}, bf16[1280,864]{0,1:T(8,128)(2,1)}, u32[]{:S(2)}) copy-start(bf16[1280,864]{0,1:T(8,128)(2,1)} %param.15) | copy-start | bytes 6635524
  64.4 1.6 %copy-start.9 = (bf16[1280,864]{0,1:T(8,128)(2,1)S(1)}, bf16[1280,864]{0,1:T(8,128)(2,1)}, u32[]{:S(2)}) copy-start(bf16[1280,864]{0,1:T(8,128)(2,1)} %param.16) | copy-start | bytes 6635524
  66.0 1.6 %copy-start.11 = (bf16[864,1280]{1,0:T(8,128)(2,1)S(1)}, bf16[864,1280]{1,0:T(8,128)(2,1)}, u32[]{:S(2)}) copy-start(bf16[864,1280]{1,0:T(8,128)(2,1)} %refs_5_.1) | copy-start | bytes 6635524
  82.4 13.3 %collective-permute-start.16 = (bf16[136,1280]{1,0:T(8,128)(2,1)S(1)}, bf16[136,1280]{1,0:T(8,128)(2,1)S(1)}, u32[]{:S(2)}, u32[]{:S(2)}) collective-permute-start(bf16[136,1280]{1,0:T(8,128)(2,1)S(1)} %get-tuple-element.140), channel_id=1, source_target_pairs={{0,3},{1,0},{2,1},{3,2},{4,7},{5,4},{6,5},{7,6},{8,11},{9,8},{10,9... | collective-permute-start | bytes 1044488 | tf_op jit(solution)/shard_map/ppermute | solution.py:32
  83.6 12.0 %collective-permute-start.17 = (bf16[136,1280]{1,0:T(8,128)(2,1)S(1)}, bf16[136,1280]{1,0:T(8,128)(2,1)S(1)}, u32[]{:S(2)}, u32[]{:S(2)}) collective-permute-start(bf16[136,1280]{1,0:T(8,128)(2,1)S(1)} %get-tuple-element.139), channel_id=1, source_target_pairs={{0,1},{1,2},{2,3},{3,0},{4,5},{5,6},{6,7},{7,4},{8,9},{9,10},{10,1... | collective-permute-start | bytes 1044488 | tf_op jit(solution)/shard_map/ppermute | solution.py:32
  85.7 15.8 %copy-start.16 = (bf16[2,72,1280]{2,1,0:T(8,128)(2,1)S(1)}, bf16[2,72,1280]{2,1,0:T(8,128)(2,1)}, u32[]{:S(2)}) copy-start(bf16[2,72,1280]{2,1,0:T(8,128)(2,1)} %copy-done.15) | copy-start | bytes 1105924
  95.5 5.9 %copy-start.12 = (bf16[864,1280]{1,0:T(8,128)(2,1)S(1)}, bf16[864,1280]{1,0:T(8,128)(2,1)}, u32[]{:S(2)}) copy-start(bf16[864,1280]{1,0:T(8,128)(2,1)} %refs_5_.1) | copy-start | bytes 6635524
  95.6 5.8 %copy-start.14 = (bf16[2,72,1280]{2,1,0:T(8,128)(2,1)S(1)}, bf16[2,72,1280]{2,1,0:T(8,128)(2,1)}, u32[]{:S(2)}) copy-start(bf16[2,72,1280]{2,1,0:T(8,128)(2,1)} %copy-done.13) | copy-start | bytes 1105924
  95.7 5.8 %copy-start.8 = (bf16[1280,864]{0,1:T(8,128)(2,1)S(1)}, bf16[1280,864]{0,1:T(8,128)(2,1)}, u32[]{:S(2)}) copy-start(bf16[1280,864]{0,1:T(8,128)(2,1)} %param.15) | copy-start | bytes 6635524
  95.7 5.8 %copy-start.10 = (bf16[1280,864]{0,1:T(8,128)(2,1)S(1)}, bf16[1280,864]{0,1:T(8,128)(2,1)}, u32[]{:S(2)}) copy-start(bf16[1280,864]{0,1:T(8,128)(2,1)} %param.16) | copy-start | bytes 6635524
  95.8 20.6 %collective-permute-start.19 = (bf16[2,136,1280]{2,1,0:T(8,128)(2,1)S(1)}, bf16[2,136,1280]{2,1,0:T(8,128)(2,1)S(1)}, u32[]{:S(2)}, u32[]{:S(2)}) collective-permute-start(bf16[2,136,1280]{2,1,0:T(8,128)(2,1)S(1)} %pad_maximum_fusion.1), channel_id=1, source_target_pairs={{0,1},{1,2},{2,3},{3,0},{4,5},{5,6},{6,7},{7,4},{8,9},{9,10},{10,1... | collective-permute-start | bytes 2088968 | tf_op jit(solution)/shard_map/ppermute | solution.py:32
  96.8 19.6 %collective-permute-start.18 = (bf16[2,136,1280]{2,1,0:T(8,128)(2,1)S(1)}, bf16[2,136,1280]{2,1,0:T(8,128)(2,1)S(1)}, u32[]{:S(2)}, u32[]{:S(2)}) collective-permute-start(bf16[2,136,1280]{2,1,0:T(8,128)(2,1)S(1)} %pad_maximum_fusion), channel_id=1, source_target_pairs={{0,3},{1,0},{2,1},{3,2},{4,7},{5,4},{6,5},{7,6},{8,11},{9,8},{10,9... | collective-permute-start | bytes 2088968 | tf_op jit(solution)/shard_map/ppermute | solution.py:32
  98.1 18.3 %collective-permute-start.20 = (bf16[72,1280]{1,0:T(8,128)(2,1)S(1)}, bf16[72,1280]{1,0:T(8,128)(2,1)S(1)}, u32[]{:S(2)}, u32[]{:S(2)}) collective-permute-start(bf16[72,1280]{1,0:T(8,128)(2,1)S(1)} %get-tuple-element.142), channel_id=1, source_target_pairs={{0,3},{1,0},{2,1},{3,2},{4,7},{5,4},{6,5},{7,6},{8,11},{9,8},{10,9... | collective-permute-start | bytes 552968 | tf_op jit(solution)/shard_map/ppermute | solution.py:32
  98.2 18.2 %collective-permute-start.21 = (bf16[72,1280]{1,0:T(8,128)(2,1)S(1)}, bf16[72,1280]{1,0:T(8,128)(2,1)S(1)}, u32[]{:S(2)}, u32[]{:S(2)}) collective-permute-start(bf16[72,1280]{1,0:T(8,128)(2,1)S(1)} %get-tuple-element.141), channel_id=1, source_target_pairs={{0,1},{1,2},{2,3},{3,0},{4,5},{5,6},{6,7},{7,4},{8,9},{9,10},{10,1... | collective-permute-start | bytes 552968 | tf_op jit(solution)/shard_map/ppermute | solution.py:32
  116.5 14.4 %collective-permute-start.23 = (bf16[2,72,1280]{2,1,0:T(8,128)(2,1)S(1)}, bf16[2,72,1280]{2,1,0:T(8,128)(2,1)S(1)}, u32[]{:S(2)}, u32[]{:S(2)}) collective-permute-start(bf16[2,72,1280]{2,1,0:T(8,128)(2,1)S(1)} %pad_maximum_fusion.2), channel_id=1, source_target_pairs={{0,3},{1,0},{2,1},{3,2},{4,7},{5,4},{6,5},{7,6},{8,11},{9,8},{10,9... | collective-permute-start | bytes 1105928 | tf_op jit(solution)/shard_map/ppermute | solution.py:32
  117.7 19.8 %copy-start.3 = (bf16[2560,4]{0,1:T(4,128)(2,1)S(1)}, bf16[2560,4]{0,1:T(4,128)(2,1)}, u32[]{:S(2)}) copy-start(bf16[2560,4]{0,1:T(4,128)(2,1)} %param.14) | copy-start | bytes 61444
  117.7 19.8 %copy-start.5 = (s32[1,128,2]{1,2,0:T(2,128)S(1)}, s32[1,128,2]{1,2,0:T(2,128)}, u32[]{:S(2)}) copy-start(s32[1,128,2]{1,2,0:T(2,128)} %param.18) | copy-start | bytes 3076
  117.7 19.8 %copy-start.6 = (s32[1,128,2]{1,2,0:T(2,128)S(1)}, s32[1,128,2]{1,2,0:T(2,128)}, u32[]{:S(2)}) copy-start(s32[1,128,2]{1,2,0:T(2,128)} %param.19) | copy-start | bytes 3076
  117.7 13.2 %collective-permute-start.24 = (bf16[2,72,1280]{2,1,0:T(8,128)(2,1)S(1)}, bf16[2,72,1280]{2,1,0:T(8,128)(2,1)S(1)}, u32[]{:S(2)}, u32[]{:S(2)}) collective-permute-start(bf16[2,72,1280]{2,1,0:T(8,128)(2,1)S(1)} %pad_maximum_fusion.3), channel_id=1, source_target_pairs={{0,1},{1,2},{2,3},{3,0},{4,5},{5,6},{6,7},{7,4},{8,9},{9,10},{10,1... | collective-permute-start | bytes 1105928 | tf_op jit(solution)/shard_map/ppermute | solution.py:32
  120.3 26.3 %copy-start.2 = (bf16[1,128,2560]{2,1,0:T(8,128)(2,1)S(1)}, bf16[1,128,2560]{2,1,0:T(8,128)(2,1)}, u32[]{:S(2)}) copy-start(bf16[1,128,2560]{2,1,0:T(8,128)(2,1)} %param.10) | copy-start | bytes 1966084
  120.4 10.7 %collective-permute-start.25 = (bf16[2,68,1280]{2,1,0:T(8,128)(2,1)S(1)}, bf16[2,68,1280]{2,1,0:T(8,128)(2,1)S(1)}, u32[]{:S(2)}, u32[]{:S(2)}) collective-permute-start(bf16[2,68,1280]{2,1,0:T(8,128)(2,1)S(1)} %get-tuple-element.138), channel_id=1, source_target_pairs={{0,12},{1,13},{2,14},{3,15},{4,0},{5,1},{6,2},{7,3},{8,4},{9,5},{1... | collective-permute-start | bytes 1044488 | tf_op jit(solution)/shard_map/ppermute | solution.py:32
  121.6 12.7 %collective-permute-start.26 = (bf16[2,68,1280]{2,1,0:T(8,128)(2,1)S(1)}, bf16[2,68,1280]{2,1,0:T(8,128)(2,1)S(1)}, u32[]{:S(2)}, u32[]{:S(2)}) collective-permute-start(bf16[2,68,1280]{2,1,0:T(8,128)(2,1)S(1)} %get-tuple-element.137), channel_id=1, source_target_pairs={{0,4},{1,5},{2,6},{3,7},{4,8},{5,9},{6,10},{7,11},{8,12},{9,13},{1... | collective-permute-start | bytes 1044488 | tf_op jit(solution)/shard_map/ppermute | solution.py:32
  122.5 15.4 %collective-permute-start.22 = (bf16[2,72,1280]{2,1,0:T(8,128)(2,1)S(1)}, bf16[2,72,1280]{2,1,0:T(8,128)(2,1)S(1)}, u32[]{:S(2)}, u32[]{:S(2)}) collective-permute-start(bf16[2,72,1280]{2,1,0:T(8,128)(2,1)S(1)} %get-tuple-element.121), channel_id=1, source_target_pairs={{0,2},{1,3},{2,0},{3,1},{4,6},{5,7},{6,4},{7,5},{8,10},{9,11},{10,... | collective-permute-start | bytes 1105928 | tf_op jit(solution)/shard_map/ppermute | solution.py:32
  134.3 8.7 %collective-permute-start.27 = (bf16[2,72,1280]{2,1,0:T(8,128)(2,1)S(1)}, bf16[2,72,1280]{2,1,0:T(8,128)(2,1)S(1)}, u32[]{:S(2)}, u32[]{:S(2)}) collective-permute-start(bf16[2,72,1280]{2,1,0:T(8,128)(2,1)S(1)} %get-tuple-element.132), channel_id=1, source_target_pairs={{0,3},{1,0},{2,1},{3,2},{4,7},{5,4},{6,5},{7,6},{8,11},{9,8},{10,9... | collective-permute-start | bytes 1105928 | tf_op jit(solution)/shard_map/ppermute | solution.py:32
  134.3 8.7 %collective-permute-start.28 = (bf16[2,72,1280]{2,1,0:T(8,128)(2,1)S(1)}, bf16[2,72,1280]{2,1,0:T(8,128)(2,1)S(1)}, u32[]{:S(2)}, u32[]{:S(2)}) collective-permute-start(bf16[2,72,1280]{2,1,0:T(8,128)(2,1)S(1)} %get-tuple-element.133), channel_id=1, source_target_pairs={{0,1},{1,2},{2,3},{3,0},{4,5},{5,6},{6,7},{7,4},{8,9},{9,10},{10,1... | collective-permute-start | bytes 1105928 | tf_op jit(solution)/shard_map/ppermute | solution.py:32
  137.5 9.0 %collective-permute-start.29 = (bf16[2,72,1280]{2,1,0:T(8,128)(2,1)S(1)}, bf16[2,72,1280]{2,1,0:T(8,128)(2,1)S(1)}, u32[]{:S(2)}, u32[]{:S(2)}) collective-permute-start(bf16[2,72,1280]{2,1,0:T(8,128)(2,1)S(1)} %add_convert_fusion.1), channel_id=1, source_target_pairs={{0,8},{1,9},{2,10},{3,11},{4,12},{5,13},{6,14},{7,15},{8,0},{9,1},... | collective-permute-start | bytes 1105928 | tf_op jit(solution)/shard_map/ppermute | solution.py:32
  (1 other events, 0.7 us)
